TPU v7x, 256 devices: a whole 4x4x8 slice. The times are simulated.
256 devices in a mesh: ctx: 32 (over x, y, core), head: 8 (over z).
Axes of the slice: x: 4, y: 4, z: 8, core: 2. Of those that a mesh axis runs over, the one named last changes fastest.
Arguments:
- queries: bfloat16 [8192, 64, 128], P('ctx', 'head'), may hold values from -130 to 130
- keys: bfloat16 [8192, 8, 128], P(('ctx', 'head')), may hold values from -5 to 5
- values: bfloat16 [8192, 8, 128], P(('ctx', 'head')), may hold values from -5 to 5
- output: bfloat16 [8192, 64, 128], P('ctx', 'head'), may hold values from -5 to 5
- grad_output: bfloat16 [8192, 64, 128], P('ctx', 'head'), may hold values from -5 to 5
- doc_lengths: int32 [16], replicated, may hold values from 1 to 1024, 8192 in all
Outputs:
- grad_queries: bfloat16 [8192, 64, 128], P('ctx', 'head')
- grad_keys: bfloat16 [8192, 8, 128], P(('ctx', 'head'))
- grad_values: bfloat16 [8192, 8, 128], P(('ctx', 'head'))
Inputs may be any that keep to these rules, and one draw needn't show every extreme that they name: `doc_lengths`: 16 positive lengths summing to 8192; the longest is exactly 1024.
All inputs are finite; a program needn't handle non-finite values.
Results may differ from a plain program's by a relative error of at most 0.0085.
Values may be sent and summed in bfloat16 or wider, within the bound.
A program may use at most 64 MiB of HBM per device.

v0:
```python
import jax
import jax.numpy as jnp
from jax import lax
from jax.sharding import PartitionSpec as P

REACH = 4


def passed_along(value, axis, steps):
    count = lax.axis_size(axis)
    leading, last = (max(0, -steps), min(count, count - steps))
    return lax.ppermute(value, axis, [(source, source + steps) for source in range(leading, last)])


def segment_of(doc_lengths, positions):
    ends = jnp.cumsum(doc_lengths)
    return jnp.sum((ends[None, :] <= positions[:, None]).astype(jnp.int32), axis=1)


def body(queries, keys, values, output, grad_output, doc_lengths):
    block_len = queries.shape[0]
    local_heads = queries.shape[1]
    width = queries.shape[2]
    local_groups = keys.shape[1] // lax.axis_size("head")
    per_group = local_heads // local_groups
    softmax_scale = 1.0 / width**0.5
    device = lax.axis_index("ctx")
    query_pos = device * block_len + jnp.arange(block_len, dtype=jnp.int32)
    asking_document_label = segment_of(doc_lengths, query_pos)
    piece_keys = [keys]
    piece_values = [values]
    for distance in range(1, REACH + 1):
        moved_keys, moved_values = passed_along((keys, values), "ctx", distance)
        piece_keys.append(moved_keys)
        piece_values.append(moved_values)
    all_keys, all_values = (
        lax.all_to_all(jnp.stack(piece_keys), "head", split_axis=2, concat_axis=1, tiled=True),
        lax.all_to_all(jnp.stack(piece_values), "head", split_axis=2, concat_axis=1, tiled=True),
    )
    window_keys = [all_keys[distance] for distance in range(REACH + 1)]
    window_values = [all_values[distance] for distance in range(REACH + 1)]
    query_row_block = queries.reshape(block_len, local_groups, per_group, width)
    gradient_row_block = grad_output.reshape(block_len, local_groups, per_group, width)
    output_row_block = output.reshape(block_len, local_groups, per_group, width)
    row_correction = jnp.einsum(
        "epvx,epvx->pve", gradient_row_block, output_row_block, preferred_element_type=jnp.float32
    )

    def block_mask(distance):
        key_start = (device - distance) * block_len
        key_pos = key_start + jnp.arange(block_len, dtype=jnp.int32)
        key_seg = segment_of(doc_lengths, key_pos)
        allowed = (
            (asking_document_label[:, None] == key_seg[None, :])
            & (key_pos[None, :] <= query_pos[:, None])
            & (key_pos[None, :] >= 0)
        )
        last_seg = segment_of(doc_lengths, jnp.reshape(key_start + block_len - 1, (1,)))[0]
        live = (device - distance >= 0) & (last_seg >= asking_document_label[0])
        return (allowed, live)

    def block_scores(distance, allowed):
        logit_matrix = (
            jnp.einsum(
                "expu,axu->xpea",
                query_row_block,
                window_keys[distance],
                preferred_element_type=jnp.float32,
            )
            * softmax_scale
        )
        return jnp.where(allowed, logit_matrix, -1e30)

    masks = [block_mask(distance) for distance in range(REACH + 1)]
    running_max = jnp.full((local_groups, per_group, block_len), -1e30, jnp.float32)
    running_sum = jnp.zeros((local_groups, per_group, block_len), jnp.float32)
    for distance in range(REACH + 1):
        allowed, live = masks[distance]

        def update_stats(state, distance=distance, allowed=allowed):
            old_max, old_sum = state
            logit_matrix = block_scores(distance, allowed)
            new_max = jnp.maximum(old_max, jnp.max(logit_matrix, axis=-1))
            new_sum = old_sum * jnp.exp(old_max - new_max) + jnp.sum(
                jnp.exp(logit_matrix - new_max[..., None]), axis=-1
            )
            return (new_max, new_sum)

        if distance == 0:
            running_max, running_sum = update_stats((running_max, running_sum))
        else:
            running_max, running_sum = lax.cond(
                live, update_stats, lambda state: state, (running_max, running_sum)
            )
    row_lse = running_max + jnp.log(running_sum)
    query_gradient = jnp.zeros((block_len, local_groups, per_group, width), jnp.float32)
    zero_part = jnp.zeros((block_len, local_groups, width), jnp.float32)
    key_parts = []
    value_parts = []
    for distance in range(REACH + 1):
        allowed, live = masks[distance]

        def gradients(accum, distance=distance, allowed=allowed):
            logit_matrix = block_scores(distance, allowed)
            probs = jnp.where(allowed, jnp.exp(logit_matrix - row_lse[..., None]), 0.0)
            attention_weights_lowprec = probs.astype(jnp.bfloat16)
            content_derivative = jnp.einsum(
                "dapg,pdaf->gdf",
                attention_weights_lowprec,
                gradient_row_block,
                preferred_element_type=jnp.float32,
            )
            probability_gradient = jnp.einsum(
                "expu,axu->xpea",
                gradient_row_block,
                window_values[distance],
                preferred_element_type=jnp.float32,
            )
            similarity_derivative = (
                probs * (probability_gradient - row_correction[..., None])
            ).astype(jnp.bfloat16)
            accum = accum + jnp.einsum(
                "mlwp,pmz->wmlz",
                similarity_derivative,
                window_keys[distance],
                preferred_element_type=jnp.float32,
            )
            lookup_derivative_portion = jnp.einsum(
                "dapg,pdaf->gdf",
                similarity_derivative,
                query_row_block,
                preferred_element_type=jnp.float32,
            )
            return (accum, lookup_derivative_portion, content_derivative)

        if distance == 0:
            query_gradient, part_keys, part_values = gradients(query_gradient)
        else:
            query_gradient, part_keys, part_values = lax.cond(
                live, gradients, lambda accum: (accum, zero_part, zero_part), query_gradient
            )
        key_parts.append(part_keys)
        value_parts.append(part_values)
    stacked_keys, stacked_values = (
        lax.all_to_all(jnp.stack(key_parts), "head", split_axis=1, concat_axis=2, tiled=True),
        lax.all_to_all(jnp.stack(value_parts), "head", split_axis=1, concat_axis=2, tiled=True),
    )
    summed_keys = stacked_keys[0]
    summed_values = stacked_values[0]
    for distance in range(1, REACH + 1):
        back_keys, back_values = (
            passed_along(stacked_keys[distance].astype(jnp.bfloat16), "ctx", -distance).astype(
                jnp.float32
            ),
            passed_along(stacked_values[distance].astype(jnp.bfloat16), "ctx", -distance).astype(
                jnp.float32
            ),
        )
        summed_keys = summed_keys + back_keys
        summed_values = summed_values + back_values
    grad_queries = (
        (query_gradient * softmax_scale).astype(jnp.bfloat16).reshape(block_len, local_heads, width)
    )
    grad_keys = (summed_keys * softmax_scale).astype(jnp.bfloat16)
    grad_values = summed_values.astype(jnp.bfloat16)
    return (grad_queries, grad_keys, grad_values)


def solution(mesh):
    return jax.shard_map(
        body,
        mesh=mesh,
        in_specs=(
            P("ctx", "head", None),
            P(("ctx", "head"), None, None),
            P(("ctx", "head"), None, None),
            P("ctx", "head", None),
            P("ctx", "head", None),
            P(),
        ),
        out_specs=(
            P("ctx", "head", None),
            P(("ctx", "head"), None, None),
            P(("ctx", "head"), None, None),
        ),
        check_vma=False,
    )
```

profile of v0, /device:TPU:14, one launch (start us, length us, event | category | flops | bytes accessed | tf_op | source)
XLA Modules:
  0.0 198.8 jit_solution(4399369992113851486)
XLA Ops:
  1.6 2.9 %collective-permute-start.6 = (bf16[32,8,128]{2,0,1:T(8,128)(2,1)S(1)}, bf16[32,8,128]{2,0,1:T(8,128)(2,1)S(1)}, u32[]{:S(2)}, u32[]{:S(2)}) collective-permute-start(bf16[32,8,128]{2,0,1:T(8,128)(2,1)S(1)} %copy.155), channel_id=1, source_target_pairs={{0,24},{8,32},{16,40},{24,48},{32,56},{40,64},{48,72},{56,80},{64,... | collective-permute-start | bytes 196616 | tf_op jit(solution)/shard_map/ppermute | solution.py:12
  4.5 3.2 %collective-permute-start.5 = (bf16[32,8,128]{2,0,1:T(8,128)(2,1)S(1)}, bf16[32,8,128]{2,0,1:T(8,128)(2,1)S(1)}, u32[]{:S(2)}, u32[]{:S(2)}) collective-permute-start(bf16[32,8,128]{2,0,1:T(8,128)(2,1)S(1)} %copy.155), channel_id=1, source_target_pairs={{0,16},{8,24},{16,32},{24,40},{32,48},{40,56},{48,64},{56,72},{64,... | collective-permute-start | bytes 196616 | tf_op jit(solution)/shard_map/ppermute | solution.py:12
  7.7 2.0 %collective-permute-start.4 = (bf16[32,8,128]{2,0,1:T(8,128)(2,1)S(1)}, bf16[32,8,128]{2,0,1:T(8,128)(2,1)S(1)}, u32[]{:S(2)}, u32[]{:S(2)}) collective-permute-start(bf16[32,8,128]{2,0,1:T(8,128)(2,1)S(1)} %copy.155), channel_id=1, source_target_pairs={{0,8},{8,16},{16,24},{24,32},{32,40},{40,48},{48,56},{56,64},{64,7... | collective-permute-start | bytes 196616 | tf_op jit(solution)/shard_map/ppermute | solution.py:12
  9.8 1.9 collective-permute-start.7
  12.5 1.9 collective-permute-start
  20.6 1.9 collective-permute-start.1
  23.1 3.7 %collective-permute-done.1 = bf16[32,8,128]{2,0,1:T(8,128)(2,1)S(1)} collective-permute-done((bf16[32,8,128]{2,0,1:T(8,128)(2,1)S(1)}, bf16[32,8,128]{2,0,1:T(8,128)(2,1)S(1)}, u32[]{:S(2)}, u32[]{:S(2)}) %collective-permute-start.1) | collective-permute-done | bytes 65568 | tf_op jit(solution)/shard_map/ppermute | solution.py:12
  26.8 1.9 collective-permute-start.2
  29.4 5.4 %collective-permute-done.2 = bf16[32,8,128]{2,0,1:T(8,128)(2,1)S(1)} collective-permute-done((bf16[32,8,128]{2,0,1:T(8,128)(2,1)S(1)}, bf16[32,8,128]{2,0,1:T(8,128)(2,1)S(1)}, u32[]{:S(2)}, u32[]{:S(2)}) %collective-permute-start.2) | collective-permute-done | bytes 65568 | tf_op jit(solution)/shard_map/ppermute | solution.py:12
  34.8 1.9 collective-permute-start.3
  37.4 6.0 %collective-permute-done.3 = bf16[32,8,128]{2,0,1:T(8,128)(2,1)S(1)} collective-permute-done((bf16[32,8,128]{2,0,1:T(8,128)(2,1)S(1)}, bf16[32,8,128]{2,0,1:T(8,128)(2,1)S(1)}, u32[]{:S(2)}, u32[]{:S(2)}) %collective-permute-start.3) | collective-permute-done | bytes 65568 | tf_op jit(solution)/shard_map/ppermute | solution.py:12
  44.0 8.5 %all-to-all-start = ((bf16[5,32,8,128]{3,1,0,2:T(8,128)(2,1)}), bf16[5,32,8,128]{3,1,0,2:T(8,128)(2,1)S(1)}, u32[]{:S(2)}, u32[]{:S(2)}) async-start(bf16[5,32,8,128]{3,1,0,2:T(8,128)(2,1)} %bitcast_dynamic-update-slice_fusion.5), calls=%async_computation | async-start | bytes 655360 | tf_op jit(solution)/shard_map/all_to_all | solution.py:37
  55.1 9.8 %all-to-all-done = bf16[5,32,8,128]{3,1,0,2:T(8,128)(2,1)S(1)} async-done(((bf16[5,32,8,128]{3,1,0,2:T(8,128)(2,1)}), bf16[5,32,8,128]{3,1,0,2:T(8,128)(2,1)S(1)}, u32[]{:S(2)}, u32[]{:S(2)}) %all-to-all-start) | async-done | bytes 327712 | tf_op jit(solution)/shard_map/all_to_all | solution.py:37
  64.9 3.4 %all-to-all-start.1 = ((bf16[5,32,8,128]{3,1,0,2:T(8,128)(2,1)}), bf16[5,32,8,128]{3,1,0,2:T(8,128)(2,1)S(1)}, u32[]{:S(2)}, u32[]{:S(2)}) async-start(bf16[5,32,8,128]{3,1,0,2:T(8,128)(2,1)} %bitcast_dynamic-update-slice_fusion), calls=%async_computation.1 | async-start | bytes 655360 | tf_op jit(solution)/shard_map/all_to_all | solution.py:38
  75.4 4.1 %all-to-all-done.1 = bf16[5,32,8,128]{3,1,0,2:T(8,128)(2,1)S(1)} async-done(((bf16[5,32,8,128]{3,1,0,2:T(8,128)(2,1)}), bf16[5,32,8,128]{3,1,0,2:T(8,128)(2,1)S(1)}, u32[]{:S(2)}, u32[]{:S(2)}) %all-to-all-start.1) | async-done | bytes 327712 | tf_op jit(solution)/shard_map/all_to_all | solution.py:38
  80.0 1.5 fusion.108
  82.5 2.5 %conditional.8 = ((f32[1,8,256]{2,1,0:T(8,128)S(1)}, f32[1,8,256]{2,1,0:T(8,128)})) conditional(s32[]{:T(128)} %convert_element_type.183, (f32[1,8,256]{2,1,0:T(8,128)S(1)}, f32[1,8,256]{2,1,0:T(8,128)}) %tuple.91, (pred[256,256]{0,1:T(8,128)(4,1)}, bf16[256,1,128]{2,0,1:T(8,128)(2,1)}, bf16[256,1,8,128]{3,0,2,1:T(8,128)(2,1)S(1)}, ...), branch_computations={%region_9.10_spmd, %region_10.0_spmd} | conditional | flops 137891840 | bytes 5349484 | solution.py:92
  85.0 2.5 %conditional.9 = ((f32[1,8,256]{2,1,0:T(8,128)S(1)}, f32[1,8,256]{2,1,0:T(8,128)})) conditional(s32[]{:T(128)} %convert_element_type.181, (f32[1,8,256]{2,1,0:T(8,128)S(1)}, f32[1,8,256]{2,1,0:T(8,128)}) %get-tuple-element.457, (pred[256,256]{0,1:T(8,128)(4,1)}, bf16[256,1,128]{2,0,1:T(8,128)(2,1)}, bf16[256,1,8,128]{3,0,2,1:T(8,128)(2,1)S(1)}, ...), branch_computations={%region_14.15_spmd, %region_15.0_spmd} | conditional | flops 137891840 | bytes 5349484 | solution.py:92
  87.5 2.5 %conditional.10 = ((f32[1,8,256]{2,1,0:T(8,128)S(1)}, f32[1,8,256]{2,1,0:T(8,128)})) conditional(s32[]{:T(128)} %convert_element_type.179, (f32[1,8,256]{2,1,0:T(8,128)S(1)}, f32[1,8,256]{2,1,0:T(8,128)}) %get-tuple-element.458, (pred[256,256]{0,1:T(8,128)(4,1)}, bf16[256,1,128]{2,0,1:T(8,128)(2,1)}, bf16[256,1,8,128]{3,0,2,1:T(8,128)(2,1)S(1)}, ...), branch_computations={%region_19.20_spmd, %region_20.0_spmd} | conditional | flops 137891840 | bytes 5349484 | solution.py:92
  89.9 2.5 %conditional.11 = ((f32[1,8,256]{2,1,0:T(8,128)S(1)}, f32[1,8,256]{2,1,0:T(8,128)})) conditional(s32[]{:T(128)} %convert_element_type.177, (f32[1,8,256]{2,1,0:T(8,128)S(1)}, f32[1,8,256]{2,1,0:T(8,128)}) %get-tuple-element.459, (pred[256,256]{0,1:T(8,128)(4,1)}, bf16[256,1,128]{2,0,1:T(8,128)(2,1)S(1)}, bf16[256,1,8,128]{3,0,2,1:T(8,128)(2,1)S(1)}, ...), branch_computations={%region_24.25_spmd, %region_25.28_spmd} | conditional | flops 137891840 | bytes 5349484 | solution.py:92
  93.8 2.2 %fusion.80 = f32[5,256,1,128]{3,1,2,0:T(8,128)} fusion(f32[1,8,256,256]{2,3,1,0:T(8,128)S(1)} %get-tuple-element.406, f32[8,256]{1,0:T(8,128)} %bitcast.164, pred[256,256]{0,1:T(8,128)(4,1)} %get-tuple-element.403, bf16[256,8,128]{2,1,0:T(8,128)(2,1)} %param.26), kind=kOutput, calls=%fused_computation.122 | convolution fusion | flops 135790592 | bytes 2826240 | tf_op jit(solution)/shard_map/dapg,pdaf->gdf/dot_general | solution.py:107
  98.4 5.8 %conditional.12 = (f32[256,1,8,128]{3,0,2,1:T(8,128)S(1)}, f32[1,256,1,128]{3,1,2,0:T(8,128)S(1)}, f32[1,256,1,128]{3,1,2,0:T(8,128)}) conditional(s32[]{:T(128)} %convert_element_type.183, (f32[256,1,8,128]{0,3,2,1:T(8,128)S(1)}) %tuple.122, (pred[256,256]{0,1:T(8,128)(4,1)}, bf16[256,1,128]{2,0,1:T(8,128)(2,1)}, ...), branch_computations={%region_28.29_spmd, %region_29.30_spmd} | conditional | flops 675545088 | bytes 21512272 | solution.py:139
  99.8 1.6 fusion.20
  104.9 3.6 %conditional.13 = (f32[256,1,8,128]{3,0,2,1:T(8,128)S(1)}, f32[1,256,1,128]{3,1,2,0:T(8,128)S(1)}, f32[1,256,1,128]{3,1,2,0:T(8,128)S(1)}) conditional(s32[]{:T(128)} %convert_element_type.181, f32[256,1,8,128]{3,0,2,1:T(8,128)S(1)} %get-tuple-element.233, (pred[256,256]{0,1:T(8,128)(4,1)}, bf16[256,1,128]{2,0,1:T(8,128)(2,1)}, ...), branch_computations={%region_30.31_spmd, %region_31.32_spmd} | conditional | flops 675545088 | bytes 15220788 | solution.py:139
  105.0 1.6 fusion.35
  109.2 3.6 %conditional.14 = (f32[256,1,8,128]{3,0,2,1:T(8,128)S(1)}, f32[1,256,1,128]{3,1,2,0:T(8,128)S(1)}, f32[1,256,1,128]{3,1,2,0:T(8,128)S(1)}) conditional(s32[]{:T(128)} %convert_element_type.179, f32[256,1,8,128]{3,0,2,1:T(8,128)S(1)} %get-tuple-element.234, (pred[256,256]{0,1:T(8,128)(4,1)}, bf16[256,1,128]{2,0,1:T(8,128)(2,1)}, ...), branch_computations={%region_32.33_spmd, %region_33.34_spmd} | conditional | flops 675545088 | bytes 15220788 | solution.py:139
  109.3 1.6 fusion.50
  113.5 3.5 %conditional.15 = (f32[256,1,8,128]{3,0,2,1:T(8,128)S(1)}, f32[1,256,1,128]{3,1,2,0:T(8,128)S(1)}, f32[1,256,1,128]{3,1,2,0:T(8,128)S(1)}) conditional(s32[]{:T(128)} %convert_element_type.177, f32[256,1,8,128]{3,0,2,1:T(8,128)S(1)} %get-tuple-element.235, (pred[256,256]{0,1:T(8,128)(4,1)}, bf16[256,1,128]{2,0,1:T(8,128)(2,1)S(1)}, ...), branch_computations={%region_34.35_spmd, %region_35.36_spmd} | conditional | flops 675545088 | bytes 14958616 | solution.py:139
  113.6 1.5 fusion.65
  117.1 1.7 constant_dynamic-update-slice_fusion.7
  118.8 1.5 constant_dynamic-update-slice_fusion.6
  120.3 1.6 constant_dynamic-update-slice_fusion.5
  122.6 2.6 %copy.179 = f32[5,256,1,128]{3,2,0,1:T(1,128)} copy(f32[5,256,1,128]{3,1,2,0:T(8,128)} %constant_dynamic-update-slice_fusion.4) | data formatting | bytes 1310720 | tf_op jit(solution)/shard_map/stack | solution.py:146
  125.2 3.5 %all-to-all-start.3 = ((f32[5,256,1,128]{3,2,0,1:T(1,128)}), f32[5,256,1,128]{3,2,0,1:T(1,128)S(1)}, u32[]{:S(2)}, u32[]{:S(2)}) async-start(f32[5,256,1,128]{3,2,0,1:T(1,128)} %copy.179), calls=%async_computation.3 | async-start | bytes 1310720 | tf_op jit(solution)/shard_map/all_to_all | solution.py:146
  129.8 1.5 copy.172
  131.3 13.8 %all-to-all-done.3 = f32[5,256,1,128]{3,2,0,1:T(1,128)S(1)} async-done(((f32[5,256,1,128]{3,2,0,1:T(1,128)}), f32[5,256,1,128]{3,2,0,1:T(1,128)S(1)}, u32[]{:S(2)}, u32[]{:S(2)}) %all-to-all-start.3) | async-done | bytes 655392 | tf_op jit(solution)/shard_map/all_to_all | solution.py:146
  145.1 3.5 %all-to-all-start.2 = ((f32[5,256,1,128]{3,2,0,1:T(1,128)}), f32[5,256,1,128]{3,2,0,1:T(1,128)S(1)}, u32[]{:S(2)}, u32[]{:S(2)}) async-start(f32[5,256,1,128]{3,2,0,1:T(1,128)} %copy.172), calls=%async_computation.2 | async-start | bytes 1310720 | tf_op jit(solution)/shard_map/all_to_all | solution.py:145
  150.2 13.0 %all-to-all-done.2 = f32[5,256,1,128]{3,2,0,1:T(1,128)S(1)} async-done(((f32[5,256,1,128]{3,2,0,1:T(1,128)}), f32[5,256,1,128]{3,2,0,1:T(1,128)S(1)}, u32[]{:S(2)}, u32[]{:S(2)}) %all-to-all-start.2) | async-done | bytes 655392 | tf_op jit(solution)/shard_map/all_to_all | solution.py:145
  163.4 4.6 %collective-permute-start.12 = (bf16[32,8,128]{2,0,1:T(8,128)(2,1)S(1)}, bf16[32,8,128]{2,0,1:T(8,128)(2,1)S(1)}, u32[]{:S(2)}, u32[]{:S(2)}) collective-permute-start(bf16[32,8,128]{2,0,1:T(8,128)(2,1)S(1)} %get-tuple-element.387), channel_id=1, source_target_pairs={{8,0},{16,8},{24,16},{32,24},{40,32},{48,40},{56,48},{64,56},{72,6... | collective-permute-start | bytes 196616 | tf_op jit(solution)/shard_map/ppermute | solution.py:12
  168.0 1.9 collective-permute-start.14
  169.9 2.3 %collective-permute-start.13 = (bf16[32,8,128]{2,0,1:T(8,128)(2,1)S(1)}, bf16[32,8,128]{2,0,1:T(8,128)(2,1)S(1)}, u32[]{:S(2)}, u32[]{:S(2)}) collective-permute-start(bf16[32,8,128]{2,0,1:T(8,128)(2,1)S(1)} %get-tuple-element.389), channel_id=1, source_target_pairs={{16,0},{24,8},{32,16},{40,24},{48,32},{56,40},{64,48},{72,56},{80,... | collective-permute-start | bytes 196616 | tf_op jit(solution)/shard_map/ppermute | solution.py:12
  172.2 11.2 %collective-permute-start.15 = (bf16[32,8,128]{2,0,1:T(8,128)(2,1)S(1)}, bf16[32,8,128]{2,0,1:T(8,128)(2,1)S(1)}, u32[]{:S(2)}, u32[]{:S(2)}) collective-permute-start(bf16[32,8,128]{2,0,1:T(8,128)(2,1)S(1)} %slice_bitcast_fusion.2), channel_id=1, source_target_pairs={{32,0},{40,8},{48,16},{56,24},{64,32},{72,40},{80,48},{88,56},{96,... | collective-permute-start | bytes 196616 | tf_op jit(solution)/shard_map/ppermute | solution.py:12
  183.4 2.0 %collective-permute-start.8 = (bf16[32,8,128]{2,0,1:T(8,128)(2,1)S(1)}, bf16[32,8,128]{2,0,1:T(8,128)(2,1)S(1)}, u32[]{:S(2)}, u32[]{:S(2)}) collective-permute-start(bf16[32,8,128]{2,0,1:T(8,128)(2,1)S(1)} %get-tuple-element.390), channel_id=1, source_target_pairs={{8,0},{16,8},{24,16},{32,24},{40,32},{48,40},{56,48},{64,56},{72,6... | collective-permute-start | bytes 196616 | tf_op jit(solution)/shard_map/ppermute | solution.py:12
  185.4 1.9 collective-permute-start.10
  187.4 3.0 %collective-permute-start.9 = (bf16[32,8,128]{2,0,1:T(8,128)(2,1)S(1)}, bf16[32,8,128]{2,0,1:T(8,128)(2,1)S(1)}, u32[]{:S(2)}, u32[]{:S(2)}) collective-permute-start(bf16[32,8,128]{2,0,1:T(8,128)(2,1)S(1)} %get-tuple-element.392), channel_id=1, source_target_pairs={{16,0},{24,8},{32,16},{40,24},{48,32},{56,40},{64,48},{72,56},{80,... | collective-permute-start | bytes 196616 | tf_op jit(solution)/shard_map/ppermute | solution.py:12
  190.4 1.9 collective-permute-start.11
  193.1 1.8 collective-permute-done.9
  194.9 3.2 %collective-permute-done.11 = bf16[32,8,128]{2,0,1:T(8,128)(2,1)S(1)} collective-permute-done((bf16[32,8,128]{2,0,1:T(8,128)(2,1)S(1)}, bf16[32,8,128]{2,0,1:T(8,128)(2,1)S(1)}, u32[]{:S(2)}, u32[]{:S(2)}) %collective-permute-start.11) | collective-permute-done | bytes 65568 | tf_op jit(solution)/shard_map/ppermute | solution.py:12
  (184 shorter events, 46.8 us)
Async XLA Ops:
  0.6 67.7 %copy-start = (bf16[256,8,128]{2,1,0:T(8,128)(2,1)S(1)}, bf16[256,8,128]{2,1,0:T(8,128)(2,1)}, u32[]{:S(2)}) copy-start(bf16[256,8,128]{2,1,0:T(8,128)(2,1)} %param.26) | copy-start | bytes 1572868
  0.6 67.7 %copy-start.16 = (bf16[256,8,128]{2,1,0:T(8,128)(2,1)S(1)}, bf16[256,8,128]{2,1,0:T(8,128)(2,1)}, u32[]{:S(2)}) copy-start(bf16[256,8,128]{2,1,0:T(8,128)(2,1)} %param.25) | copy-start | bytes 1572868
  1.6 52.2 %collective-permute-start.6 = (bf16[32,8,128]{2,0,1:T(8,128)(2,1)S(1)}, bf16[32,8,128]{2,0,1:T(8,128)(2,1)S(1)}, u32[]{:S(2)}, u32[]{:S(2)}) collective-permute-start(bf16[32,8,128]{2,0,1:T(8,128)(2,1)S(1)} %copy.155), channel_id=1, source_target_pairs={{0,24},{8,32},{16,40},{24,48},{32,56},{40,64},{48,72},{56,80},{64,... | collective-permute-start | bytes 196616 | tf_op jit(solution)/shard_map/ppermute | solution.py:12
  4.5 48.6 %collective-permute-start.5 = (bf16[32,8,128]{2,0,1:T(8,128)(2,1)S(1)}, bf16[32,8,128]{2,0,1:T(8,128)(2,1)S(1)}, u32[]{:S(2)}, u32[]{:S(2)}) collective-permute-start(bf16[32,8,128]{2,0,1:T(8,128)(2,1)S(1)} %copy.155), channel_id=1, source_target_pairs={{0,16},{8,24},{16,32},{24,40},{32,48},{40,56},{48,64},{56,72},{64,... | collective-permute-start | bytes 196616 | tf_op jit(solution)/shard_map/ppermute | solution.py:12
  7.7 44.8 %collective-permute-start.4 = (bf16[32,8,128]{2,0,1:T(8,128)(2,1)S(1)}, bf16[32,8,128]{2,0,1:T(8,128)(2,1)S(1)}, u32[]{:S(2)}, u32[]{:S(2)}) collective-permute-start(bf16[32,8,128]{2,0,1:T(8,128)(2,1)S(1)} %copy.155), channel_id=1, source_target_pairs={{0,8},{8,16},{16,24},{24,32},{32,40},{40,48},{48,56},{56,64},{64,7... | collective-permute-start | bytes 196616 | tf_op jit(solution)/shard_map/ppermute | solution.py:12
  9.8 44.7 %collective-permute-start.7 = (bf16[32,8,128]{2,0,1:T(8,128)(2,1)S(1)}, bf16[32,8,128]{2,0,1:T(8,128)(2,1)S(1)}, u32[]{:S(2)}, u32[]{:S(2)}) collective-permute-start(bf16[32,8,128]{2,0,1:T(8,128)(2,1)S(1)} %copy.155), channel_id=1, source_target_pairs={{0,32},{8,40},{16,48},{24,56},{32,64},{40,72},{48,80},{56,88},{64,... | collective-permute-start | bytes 196616 | tf_op jit(solution)/shard_map/ppermute | solution.py:12
  12.5 8.0 %collective-permute-start = (bf16[32,8,128]{2,0,1:T(8,128)(2,1)S(1)}, bf16[32,8,128]{2,0,1:T(8,128)(2,1)S(1)}, u32[]{:S(2)}, u32[]{:S(2)}) collective-permute-start(bf16[32,8,128]{2,0,1:T(8,128)(2,1)S(1)} %copy.148), channel_id=1, source_target_pairs={{0,8},{8,16},{16,24},{24,32},{32,40},{40,48},{48,56},{56,64},{64,7... | collective-permute-start | bytes 196616 | tf_op jit(solution)/shard_map/ppermute | solution.py:12
  17.7 56.8 %copy-start.5 = (bf16[256,8,128]{2,1,0:T(8,128)(2,1)S(1)}, bf16[256,8,128]{2,1,0:T(8,128)(2,1)}, u32[]{:S(2)}) copy-start(bf16[256,8,128]{2,1,0:T(8,128)(2,1)} %param.22) | copy-start | bytes 1572868
  20.6 6.3 %collective-permute-start.1 = (bf16[32,8,128]{2,0,1:T(8,128)(2,1)S(1)}, bf16[32,8,128]{2,0,1:T(8,128)(2,1)S(1)}, u32[]{:S(2)}, u32[]{:S(2)}) collective-permute-start(bf16[32,8,128]{2,0,1:T(8,128)(2,1)S(1)} %copy.148), channel_id=1, source_target_pairs={{0,16},{8,24},{16,32},{24,40},{32,48},{40,56},{48,64},{56,72},{64,... | collective-permute-start | bytes 196616 | tf_op jit(solution)/shard_map/ppermute | solution.py:12
  26.8 8.0 %collective-permute-start.2 = (bf16[32,8,128]{2,0,1:T(8,128)(2,1)S(1)}, bf16[32,8,128]{2,0,1:T(8,128)(2,1)S(1)}, u32[]{:S(2)}, u32[]{:S(2)}) collective-permute-start(bf16[32,8,128]{2,0,1:T(8,128)(2,1)S(1)} %copy.148), channel_id=1, source_target_pairs={{0,24},{8,32},{16,40},{24,48},{32,56},{40,64},{48,72},{56,80},{64,... | collective-permute-start | bytes 196616 | tf_op jit(solution)/shard_map/ppermute | solution.py:12
  34.8 8.6 %collective-permute-start.3 = (bf16[32,8,128]{2,0,1:T(8,128)(2,1)S(1)}, bf16[32,8,128]{2,0,1:T(8,128)(2,1)S(1)}, u32[]{:S(2)}, u32[]{:S(2)}) collective-permute-start(bf16[32,8,128]{2,0,1:T(8,128)(2,1)S(1)} %copy.148), channel_id=1, source_target_pairs={{0,32},{8,40},{16,48},{24,56},{32,64},{40,72},{48,80},{56,88},{64,... | collective-permute-start | bytes 196616 | tf_op jit(solution)/shard_map/ppermute | solution.py:12
  44.0 20.9 %all-to-all-start = ((bf16[5,32,8,128]{3,1,0,2:T(8,128)(2,1)}), bf16[5,32,8,128]{3,1,0,2:T(8,128)(2,1)S(1)}, u32[]{:S(2)}, u32[]{:S(2)}) async-start(bf16[5,32,8,128]{3,1,0,2:T(8,128)(2,1)} %bitcast_dynamic-update-slice_fusion.5), calls=%async_computation | async-start | bytes 655360 | tf_op jit(solution)/shard_map/all_to_all | solution.py:37
  64.9 14.5 %all-to-all-start.1 = ((bf16[5,32,8,128]{3,1,0,2:T(8,128)(2,1)}), bf16[5,32,8,128]{3,1,0,2:T(8,128)(2,1)S(1)}, u32[]{:S(2)}, u32[]{:S(2)}) async-start(bf16[5,32,8,128]{3,1,0,2:T(8,128)(2,1)} %bitcast_dynamic-update-slice_fusion), calls=%async_computation.1 | async-start | bytes 655360 | tf_op jit(solution)/shard_map/all_to_all | solution.py:38
  82.5 1.4 copy-start.14
  82.5 1.9 copy-start.27
  85.0 1.4 copy-start.13
  85.0 1.9 copy-start.29
  87.5 1.4 copy-start.12
  87.5 1.9 copy-start.31
  89.9 1.4 copy-start.11
  89.9 1.9 copy-start.33
  92.4 3.6 %copy-start.1 = (bf16[256,8,128]{2,1,0:T(8,128)(2,1)S(1)}, bf16[256,8,128]{2,1,0:T(8,128)(2,1)}, u32[]{:S(2)}) copy-start(bf16[256,8,128]{2,1,0:T(8,128)(2,1)} %param.26) | copy-start | bytes 1572868
  92.4 3.6 %copy-start.15 = (pred[256,256]{0,1:T(8,128)(4,1)S(1)}, pred[256,256]{0,1:T(8,128)(4,1)}, u32[]{:S(2)}) copy-start(pred[256,256]{0,1:T(8,128)(4,1)} %get-tuple-element.403) | copy-start | bytes 196612
  92.4 3.6 %copy-start.35 = (bf16[1,8,32,1,128]{4,2,0,1,3:T(8,128)(2,1)S(1)}, bf16[1,8,32,1,128]{4,2,0,1,3:T(8,128)(2,1)}, u32[]{:S(2)}) copy-start(bf16[1,8,32,1,128]{4,2,0,1,3:T(8,128)(2,1)} %slice.124) | copy-start | bytes 196612
  96.0 1.4 copy-start.10
  97.5 1.0 copy-start.3
  102.4 1.2 copy-start.2
  102.4 1.2 copy-start.9
  107.0 0.9 copy-start.8
  111.3 0.9 copy-start.7
  112.8 0.7 copy-start.23
  117.1 5.5 %copy-start.25 = (f32[1,256,1,128]{3,1,2,0:T(8,128)}, f32[1,256,1,128]{3,1,2,0:T(8,128)S(1)}, u32[]{:S(2)}) copy-start(f32[1,256,1,128]{3,1,2,0:T(8,128)S(1)} %get-tuple-element.240) | copy-start | bytes 393220
  117.1 11.7 %copy-start.4 = (bf16[8,256,256]{1,2,0:T(8,128)(2,1)S(1)}, bf16[8,256,256]{1,2,0:T(8,128)(2,1)}, u32[]{:S(2)}) copy-start(bf16[8,256,256]{1,2,0:T(8,128)(2,1)} %copy-done.3) | copy-start | bytes 3145732
  117.1 11.7 %copy-start.6 = (bf16[256,8,128]{2,1,0:T(8,128)(2,1)S(1)}, bf16[256,8,128]{2,1,0:T(8,128)(2,1)}, u32[]{:S(2)}) copy-start(bf16[256,8,128]{2,1,0:T(8,128)(2,1)} %param.22) | copy-start | bytes 1572868
  122.6 6.7 %copy-start.18 = (f32[1,256,1,128]{3,1,2,0:T(8,128)S(1)}, f32[1,256,1,128]{3,1,2,0:T(8,128)}, u32[]{:S(2)}) copy-start(f32[1,256,1,128]{3,1,2,0:T(8,128)} %copy-done.17) | copy-start | bytes 393220
  122.6 6.7 %copy-start.21 = (f32[1,256,1,128]{3,1,2,0:T(8,128)S(1)}, f32[1,256,1,128]{3,1,2,0:T(8,128)}, u32[]{:S(2)}) copy-start(f32[1,256,1,128]{3,1,2,0:T(8,128)} %copy-done.20) | copy-start | bytes 393220
  125.2 19.8 %all-to-all-start.3 = ((f32[5,256,1,128]{3,2,0,1:T(1,128)}), f32[5,256,1,128]{3,2,0,1:T(1,128)S(1)}, u32[]{:S(2)}, u32[]{:S(2)}) async-start(f32[5,256,1,128]{3,2,0,1:T(1,128)} %copy.179), calls=%async_computation.3 | async-start | bytes 1310720 | tf_op jit(solution)/shard_map/all_to_all | solution.py:146
  128.8 0.9 copy-start.24
  128.8 1.0 copy-start.26
  145.1 18.2 %all-to-all-start.2 = ((f32[5,256,1,128]{3,2,0,1:T(1,128)}), f32[5,256,1,128]{3,2,0,1:T(1,128)S(1)}, u32[]{:S(2)}, u32[]{:S(2)}) async-start(f32[5,256,1,128]{3,2,0,1:T(1,128)} %copy.172), calls=%async_computation.2 | async-start | bytes 1310720 | tf_op jit(solution)/shard_map/all_to_all | solution.py:145
  163.4 22.0 %collective-permute-start.12 = (bf16[32,8,128]{2,0,1:T(8,128)(2,1)S(1)}, bf16[32,8,128]{2,0,1:T(8,128)(2,1)S(1)}, u32[]{:S(2)}, u32[]{:S(2)}) collective-permute-start(bf16[32,8,128]{2,0,1:T(8,128)(2,1)S(1)} %get-tuple-element.387), channel_id=1, source_target_pairs={{8,0},{16,8},{24,16},{32,24},{40,32},{48,40},{56,48},{64,56},{72,6... | collective-permute-start | bytes 196616 | tf_op jit(solution)/shard_map/ppermute | solution.py:12
  168.0 19.4 %collective-permute-start.14 = (bf16[32,8,128]{2,0,1:T(8,128)(2,1)S(1)}, bf16[32,8,128]{2,0,1:T(8,128)(2,1)S(1)}, u32[]{:S(2)}, u32[]{:S(2)}) collective-permute-start(bf16[32,8,128]{2,0,1:T(8,128)(2,1)S(1)} %get-tuple-element.388), channel_id=1, source_target_pairs={{24,0},{32,8},{40,16},{48,24},{56,32},{64,40},{72,48},{80,56},{88,... | collective-permute-start | bytes 196616 | tf_op jit(solution)/shard_map/ppermute | solution.py:12
  169.9 20.5 %collective-permute-start.13 = (bf16[32,8,128]{2,0,1:T(8,128)(2,1)S(1)}, bf16[32,8,128]{2,0,1:T(8,128)(2,1)S(1)}, u32[]{:S(2)}, u32[]{:S(2)}) collective-permute-start(bf16[32,8,128]{2,0,1:T(8,128)(2,1)S(1)} %get-tuple-element.389), channel_id=1, source_target_pairs={{16,0},{24,8},{32,16},{40,24},{48,32},{56,40},{64,48},{72,56},{80,... | collective-permute-start | bytes 196616 | tf_op jit(solution)/shard_map/ppermute | solution.py:12
  172.2 20.1 %collective-permute-start.15 = (bf16[32,8,128]{2,0,1:T(8,128)(2,1)S(1)}, bf16[32,8,128]{2,0,1:T(8,128)(2,1)S(1)}, u32[]{:S(2)}, u32[]{:S(2)}) collective-permute-start(bf16[32,8,128]{2,0,1:T(8,128)(2,1)S(1)} %slice_bitcast_fusion.2), channel_id=1, source_target_pairs={{32,0},{40,8},{48,16},{56,24},{64,32},{72,40},{80,48},{88,56},{96,... | collective-permute-start | bytes 196616 | tf_op jit(solution)/shard_map/ppermute | solution.py:12
  183.4 9.6 %collective-permute-start.8 = (bf16[32,8,128]{2,0,1:T(8,128)(2,1)S(1)}, bf16[32,8,128]{2,0,1:T(8,128)(2,1)S(1)}, u32[]{:S(2)}, u32[]{:S(2)}) collective-permute-start(bf16[32,8,128]{2,0,1:T(8,128)(2,1)S(1)} %get-tuple-element.390), channel_id=1, source_target_pairs={{8,0},{16,8},{24,16},{32,24},{40,32},{48,40},{56,48},{64,56},{72,6... | collective-permute-start | bytes 196616 | tf_op jit(solution)/shard_map/ppermute | solution.py:12
  185.4 7.6 %collective-permute-start.10 = (bf16[32,8,128]{2,0,1:T(8,128)(2,1)S(1)}, bf16[32,8,128]{2,0,1:T(8,128)(2,1)S(1)}, u32[]{:S(2)}, u32[]{:S(2)}) collective-permute-start(bf16[32,8,128]{2,0,1:T(8,128)(2,1)S(1)} %get-tuple-element.391), channel_id=1, source_target_pairs={{24,0},{32,8},{40,16},{48,24},{56,32},{64,40},{72,48},{80,56},{88,... | collective-permute-start | bytes 196616 | tf_op jit(solution)/shard_map/ppermute | solution.py:12
  187.4 7.4 %collective-permute-start.9 = (bf16[32,8,128]{2,0,1:T(8,128)(2,1)S(1)}, bf16[32,8,128]{2,0,1:T(8,128)(2,1)S(1)}, u32[]{:S(2)}, u32[]{:S(2)}) collective-permute-start(bf16[32,8,128]{2,0,1:T(8,128)(2,1)S(1)} %get-tuple-element.392), channel_id=1, source_target_pairs={{16,0},{24,8},{32,16},{40,24},{48,32},{56,40},{64,48},{72,56},{80,... | collective-permute-start | bytes 196616 | tf_op jit(solution)/shard_map/ppermute | solution.py:12
  190.4 7.7 %collective-permute-start.11 = (bf16[32,8,128]{2,0,1:T(8,128)(2,1)S(1)}, bf16[32,8,128]{2,0,1:T(8,128)(2,1)S(1)}, u32[]{:S(2)}, u32[]{:S(2)}) collective-permute-start(bf16[32,8,128]{2,0,1:T(8,128)(2,1)S(1)} %slice_bitcast_fusion.6), channel_id=1, source_target_pairs={{32,0},{40,8},{48,16},{56,24},{64,32},{72,40},{80,48},{88,56},{96,... | collective-permute-start | bytes 196616 | tf_op jit(solution)/shard_map/ppermute | solution.py:12
  (8 other events, 5.0 us)
where the time goes:
time: 201 us; the launch traced here: 199 us
  starting transfers between devices  65.5 us (33%)
  waiting for transfers between devices  60.8 us (30%)
  local copies, waits for them, and re-layouts  31.1 us (15%)
  matrix products  26 us (13%)
  other arithmetic  8.58 us (4%)
  between operations  6.46 us (3%)
    ppermute x16, starting transfers between devices, passed_along(): lax.ppermute(value, axis, [(source, source + steps) for source in range(l...  46.5 us
    ppermute x16, waiting for transfers between devices, passed_along(): lax.ppermute(value, axis, [(source, source + steps) for source in range(l...  20.1 us
    unnamed x58, local copies, waits for them, and re-layouts  17.9 us
    all_to_all x1, waiting for transfers between devices, body(): lax.all_to_all(jnp.stack(value_parts), 'head', split_axis=1, concat_axis=...  13.8 us
    dot_general x9, matrix products, block_scores(): jnp.einsum('expu,axu->xpea', query_row_block, window_keys[distance], pref...  13.2 us
    all_to_all x1, waiting for transfers between devices, body(): lax.all_to_all(jnp.stack(key_parts), 'head', split_axis=1, concat_axis=2,...  13 us
    all_to_all x1, waiting for transfers between devices, body(): lax.all_to_all(jnp.stack(piece_keys), 'head', split_axis=2, concat_axis=1...  9.81 us
    all_to_all x1, starting transfers between devices, body(): lax.all_to_all(jnp.stack(piece_keys), 'head', split_axis=2, concat_axis=1...  8.47 us
  transfers between devices with their start and end apart: 20, of which 9 were waited for; matrix products, arithmetic and copies ran while one was open for 9% of the time, Pallas kernels for 0%

commit v1 on v0

v1 whole, which is shorter than its diff:
```python
import functools
import math

import jax
import jax.numpy as jnp
from jax import lax
from jax.experimental import pallas as pl
from jax.experimental.pallas import tpu as pltpu
from jax.sharding import PartitionSpec as P

MESH = pl.DeviceIdType.MESH
F32 = jnp.float32
BF16 = jnp.bfloat16

BLOCK = 256
REACH = 4
WINDOW = (REACH + 1) * BLOCK
WIDTH = 128
HEADS = 8
GROUPS = 8
ROWS = BLOCK * HEADS
TILE = 256
TILES = ROWS // TILE
STEP = TILE // HEADS
BAND = REACH * BLOCK + STEP
PIECE = BLOCK // GROUPS
NDOCS = 16
FAR = 2.0**20
SCALE = 1.0 / math.sqrt(WIDTH)
RATE = SCALE / math.log(2.0)

CHUNKS = ((0, BLOCK), (BLOCK, BLOCK), (2 * BLOCK, BLOCK), (3 * BLOCK, BLOCK + STEP))

NT = (((1,), (1,)), ((), ()))
NN = (((1,), (0,)), ((), ()))
TN = (((0,), (0,)), ((), ()))


def dot(a, b, dims=NN):
    return lax.dot_general(a, b, dims, preferred_element_type=F32)


def iota(shape, dim):
    return lax.broadcasted_iota(jnp.int32, shape, dim)


def kernel(
    n_ctx,
    lens_ref, q_ref, o_ref, g_ref, k_ref, v_ref,
    dq_ref, dk_ref, dv_ref,
    kb, vb, kp, vp, kaug, qaug, gt, delta, band, m_st, l_st, w_st, wd_st,
    dka, dva, stage, got, fin, sent,
    ks_sem, kr_sem, vs_sem, vr_sem, cs_sem, cr_sem, rs_sem, rr_sem, fs_sem, fr_sem,
):
    c = lax.axis_index("ctx")
    z = lax.axis_index("head")
    core = lax.rem(c, 2)
    sib = c + 1 - 2 * core
    nxt = lax.rem(c + 2, n_ctx)
    prv = lax.rem(c + n_ctx - 2, n_ctx)
    peers = [lax.rem(z + o, GROUPS) for o in range(1, GROUPS)]

    barrier = pltpu.get_barrier_semaphore()
    for peer in peers:
        pl.semaphore_signal(barrier, inc=1, device_id={"head": peer}, device_id_type=MESH)
    for other in (sib, nxt, prv):
        pl.semaphore_signal(barrier, inc=1, device_id={"ctx": other}, device_id_type=MESH)

    row, col = iota((BLOCK, BLOCK), 0), iota((BLOCK, BLOCK), 1)
    order = jnp.where(
        col == (row % PIECE) * GROUPS + row // PIECE, 1.0, 0.0
    ).astype(BF16)
    kp[...] = dot(order, k_ref[...]).astype(BF16)
    vp[...] = dot(order, v_ref[...]).astype(BF16)

    pl.semaphore_wait(barrier, GROUPS + 2)

    mine = pl.multiple_of(PIECE * z, PIECE)
    k_copies, v_copies = [], []
    for piece, window, send, recv, copies in (
        (kp, kb, ks_sem, kr_sem, k_copies),
        (vp, vb, vs_sem, vr_sem, v_copies),
    ):
        for o, peer in enumerate(peers):
            copy = pltpu.make_async_remote_copy(
                src_ref=piece.at[pl.ds(pl.multiple_of(PIECE * peer, PIECE), PIECE)],
                dst_ref=window.at[pl.ds(pl.multiple_of(REACH * BLOCK + mine, PIECE), PIECE)],
                send_sem=send.at[o],
                recv_sem=recv.at[o],
                device_id={"head": peer},
                device_id_type=MESH,
            )
            copy.start()
            copies.append(copy)
        window[pl.ds(pl.multiple_of(REACH * BLOCK + mine, PIECE), PIECE), :] = piece[pl.ds(mine, PIECE), :]

    lane = iota((1, WIDTH), 1)
    start = jnp.int32(0)
    starts = jnp.full((1, WIDTH), 1 << 30, jnp.int32)
    ends = jnp.full((1, WIDTH), 1 << 30, jnp.int32)
    for doc in range(NDOCS):
        end = start + lens_ref[doc]
        starts = jnp.where(lane == doc, start, starts)
        ends = jnp.where(lane == doc, end, ends)
        start = end
    starts = jnp.where(lane == NDOCS, -(1 << 30), starts)
    ends = jnp.where(lane == NDOCS, 0, ends)

    key_pos = (c - REACH) * BLOCK + iota((WINDOW, WIDTH), 0)
    kaug[...] = jnp.where((starts <= key_pos) & (key_pos < ends), 1.0, 0.0).astype(BF16)
    row_pos = c * BLOCK + iota((ROWS, WIDTH), 0) // HEADS
    outside = jnp.where((starts <= row_pos) & (row_pos < ends), 0.0, -FAR)
    qaug[...] = jnp.where(iota((ROWS, WIDTH), 1) <= NDOCS, outside, 0.0).astype(BF16)

    for t in range(TILES):
        g_t = jnp.transpose(g_ref[pl.ds(TILE * t, TILE), :])
        o_t = jnp.transpose(o_ref[pl.ds(TILE * t, TILE), :])
        gt[t] = g_t
        delta[pl.ds(t, 1), :] = jnp.sum(
            g_t.astype(F32) * o_t.astype(F32), axis=0, keepdims=True
        )
    dka[...] = jnp.zeros_like(dka)
    dva[...] = jnp.zeros_like(dva)

    def cross(window, i, hop):
        at = REACH * BLOCK - 2 * BLOCK * hop
        return pltpu.make_async_remote_copy(
            src_ref=window.at[pl.ds(at, BLOCK)],
            dst_ref=window.at[pl.ds(at - 2 * BLOCK, BLOCK)],
            send_sem=cs_sem.at[i, hop],
            recv_sem=cr_sem.at[i, hop],
            device_id={"ctx": nxt},
            device_id_type=MESH,
        )

    def aside(window, i, hop):
        at = (REACH - 2 * hop) * BLOCK - 2 * BLOCK * core
        return pltpu.make_async_remote_copy(
            src_ref=window.at[pl.ds(pl.multiple_of(at, BLOCK), BLOCK)],
            dst_ref=window.at[pl.ds((REACH - 2 * hop - 1) * BLOCK, BLOCK)],
            send_sem=cs_sem.at[i, 2 + hop],
            recv_sem=cr_sem.at[i, 2 + hop],
            device_id={"ctx": sib},
            device_id_type=MESH,
        )

    cross_k = [cross(kb, 0, hop) for hop in range(2)]
    cross_v = [cross(vb, 1, hop) for hop in range(2)]
    aside_k = [aside(kb, 0, hop) for hop in range(2)]
    aside_v = [aside(vb, 1, hop) for hop in range(2)]

    for copies, crossing, siding in ((k_copies, cross_k, aside_k), (v_copies, cross_v, aside_v)):
        for copy in copies:
            copy.wait_recv()
        crossing[0].start()

        @pl.when(core == 0)
        def _(siding=siding):
            siding[0].start()

    def relay(crossing, siding):
        crossing[0].wait_recv()
        crossing[1].start()

        @pl.when(core == 0)
        def _():
            siding[1].start()

        @pl.when(core == 1)
        def _():
            siding[0].start()

    def relay_last(crossing, siding):
        crossing[1].wait_recv()

        @pl.when(core == 1)
        def _():
            siding[1].start()

    def scores(b):
        off, rows = CHUNKS[b]

        def tile(t, carry):
            at = pl.ds(pl.multiple_of(STEP * t + off, STEP), rows)
            here = pl.ds(pl.multiple_of(TILE * t, TILE), TILE)
            left = jnp.concatenate([kb[at, :], kaug[at, :]], axis=1)
            right = jnp.concatenate([q_ref[here, :], qaug[here, :]], axis=1)
            s = dot(left, right, NT)
            if rows > BLOCK:
                own = jnp.where(
                    iota((STEP, TILE), 0) <= iota((STEP, TILE), 1) // HEADS, s[BLOCK:], -1e30
                )
                s = jnp.concatenate([s[:BLOCK], own], axis=0)
            m = jnp.max(s, axis=0, keepdims=True)
            e = jnp.exp2((s - m) * RATE)
            m_st[b, pl.ds(t, 1), :] = m
            l_st[b, pl.ds(t, 1), :] = jnp.sum(e, axis=0, keepdims=True)
            band[t, pl.ds(off, rows), :] = e.astype(BF16)
            return carry

        lax.fori_loop(0, TILES, tile, 0, unroll=2)

    relay(cross_k, aside_k)
    aside_k[0].wait_recv()
    scores(3)
    relay(cross_v, aside_v)
    scores(2)
    relay_last(cross_k, aside_k)
    aside_k[1].wait_recv()
    scores(1)
    relay_last(cross_v, aside_v)
    scores(0)

    top = jnp.maximum(jnp.maximum(m_st[0], m_st[1]), jnp.maximum(m_st[2], m_st[3]))
    parts = [jnp.exp2((m_st[b] - top) * RATE) for b in range(4)]
    total = sum(part * l_st[b] for b, part in enumerate(parts))
    for b, part in enumerate(parts):
        share = part / total
        w_st[b] = share
        wd_st[b] = share * delta[...]

    def grads(b):
        off, rows = CHUNKS[b]

        def tile(t, carry):
            at = pl.ds(pl.multiple_of(STEP * t + off, STEP), rows)
            here = pl.ds(pl.multiple_of(TILE * t, TILE), TILE)
            g_t = (gt[t].astype(F32) * w_st[b, pl.ds(t, 1), :]).astype(BF16)
            dp = dot(vb[at, :], g_t)
            e = band[t, pl.ds(off, rows), :]
            ds = e * (dp - wd_st[b, pl.ds(t, 1), :]).astype(BF16)
            band[t, pl.ds(off, rows), :] = ds
            dva[at, :] += dot(e, g_t, NT)
            dka[at, :] += dot(ds, q_ref[here, :])
            return carry

        lax.fori_loop(0, TILES, tile, 0, unroll=2)

    def back(i, hop, other):
        return pltpu.make_async_remote_copy(
            src_ref=stage.at[i, hop],
            dst_ref=got.at[i, hop],
            send_sem=rs_sem.at[i, hop],
            recv_sem=rr_sem.at[i, hop],
            device_id={"ctx": other},
            device_id_type=MESH,
        )

    accs = (dva, dka)
    side_b = [back(i, 0, sib) for i in range(2)]
    side_a = [back(i, 1, sib) for i in range(2)]
    far_b = [back(i, 2, prv) for i in range(2)]
    far_a = [back(i, 3, prv) for i in range(2)]

    def slot(s):
        return pl.ds(BLOCK * s, BLOCK)

    def hand(copy, i, hop, value):
        stage[i, hop] = value.astype(BF16)
        copy.start()

    aside_v[1].wait_recv()
    grads(0)
    for i in range(2):

        @pl.when(core == 0)
        def _(i=i):
            hand(far_b[i], i, 2, accs[i][slot(0), :])

    grads(1)
    for i in range(2):
        hand(side_b[i], i, 0, accs[i][slot(1), :])
    aside_v[0].wait_recv()
    grads(2)
    for i in range(2):
        side_b[i].wait_recv()

        @pl.when(core == 1)
        def _(i=i):
            hand(far_b[i], i, 2, accs[i][slot(0), :] + got[i, 0].astype(F32))

    grads(3)
    for i in range(2):
        hand(side_a[i], i, 1, accs[i][slot(3), :])
    for i in range(2):
        far_b[i].wait_recv()

        @pl.when(core == 0)
        def _(i=i):
            hand(far_a[i], i, 3, accs[i][slot(2), :] + got[i, 0].astype(F32) + got[i, 2].astype(F32))

    for i in range(2):
        side_a[i].wait_recv()

        @pl.when(core == 1)
        def _(i=i):
            hand(far_a[i], i, 3, accs[i][slot(2), :] + got[i, 1].astype(F32) + got[i, 2].astype(F32))

    def queries(t, carry):
        at = pl.ds(pl.multiple_of(STEP * t, STEP), BAND)
        here = pl.ds(pl.multiple_of(TILE * t, TILE), TILE)
        dq_ref[here, :] = (dot(band[t], kb[at, :], TN) * SCALE).astype(BF16)
        return carry

    lax.fori_loop(0, TILES, queries, 0)

    last = []
    for i in range(2):
        far_a[i].wait_recv()
        whole = accs[i][slot(4), :] + got[i, 3].astype(F32)
        whole = whole + jnp.where(core == 0, got[i, 1].astype(F32), 0.0)
        if i == 1:
            whole = whole * SCALE
        sent[i] = whole.astype(BF16)
        for o, peer in enumerate(peers):
            copy = pltpu.make_async_remote_copy(
                src_ref=sent.at[i, pl.ds(pl.multiple_of(PIECE * peer, PIECE), PIECE)],
                dst_ref=fin.at[i, pl.ds(mine, PIECE)],
                send_sem=fs_sem.at[i, o],
                recv_sem=fr_sem.at[i, o],
                device_id={"head": peer},
                device_id_type=MESH,
            )
            copy.start()
            last.append(copy)
        fin[i, pl.ds(mine, PIECE), :] = sent[i, pl.ds(mine, PIECE), :]

    place = jnp.where(
        row == (col % PIECE) * GROUPS + col // PIECE, 1.0, 0.0
    ).astype(BF16)
    for i, out_ref in enumerate((dv_ref, dk_ref)):
        for copy in last[i * (GROUPS - 1) : (i + 1) * (GROUPS - 1)]:
            copy.wait_recv()
        out_ref[...] = dot(place, fin[i]).astype(BF16)

    for copy in k_copies + v_copies + last:
        copy.wait_send()
    for group in (cross_k, cross_v, aside_k, aside_v, side_a, side_b, far_a, far_b):
        for copy in group:
            copy.wait_send()


def solution(mesh):
    n_ctx = mesh.shape["ctx"]
    dma = pltpu.SemaphoreType.DMA

    def body(queries, keys, values, output, grad_output, doc_lengths):
        flat = lambda x: x.reshape(-1, WIDTH)
        vmem = pl.BlockSpec(memory_space=pltpu.VMEM)
        piece = PIECE * GROUPS
        dq, dk, dv = pl.pallas_call(
            functools.partial(kernel, n_ctx),
            out_shape=(
                jax.ShapeDtypeStruct((ROWS, WIDTH), BF16),
                jax.ShapeDtypeStruct((piece, WIDTH), BF16),
                jax.ShapeDtypeStruct((piece, WIDTH), BF16),
            ),
            in_specs=[pl.BlockSpec(memory_space=pltpu.SMEM)] + [vmem] * 5,
            out_specs=(vmem, vmem, vmem),
            scratch_shapes=[
                pltpu.VMEM((WINDOW, WIDTH), BF16),
                pltpu.VMEM((WINDOW, WIDTH), BF16),
                pltpu.VMEM((piece, WIDTH), BF16),
                pltpu.VMEM((piece, WIDTH), BF16),
                pltpu.VMEM((WINDOW, WIDTH), BF16),
                pltpu.VMEM((ROWS, WIDTH), BF16),
                pltpu.VMEM((TILES, WIDTH, TILE), BF16),
                pltpu.VMEM((TILES, TILE), F32),
                pltpu.VMEM((TILES, BAND, TILE), BF16),
                pltpu.VMEM((4, TILES, TILE), F32),
                pltpu.VMEM((4, TILES, TILE), F32),
                pltpu.VMEM((4, TILES, TILE), F32),
                pltpu.VMEM((4, TILES, TILE), F32),
                pltpu.VMEM((WINDOW, WIDTH), F32),
                pltpu.VMEM((WINDOW, WIDTH), F32),
                pltpu.VMEM((2, 4, BLOCK, WIDTH), BF16),
                pltpu.VMEM((2, 4, BLOCK, WIDTH), BF16),
                pltpu.VMEM((2, BLOCK, WIDTH), BF16),
                pltpu.VMEM((2, BLOCK, WIDTH), BF16),
                dma((GROUPS - 1,)),
                dma((GROUPS - 1,)),
                dma((GROUPS - 1,)),
                dma((GROUPS - 1,)),
                dma((2, 4)),
                dma((2, 4)),
                dma((2, 4)),
                dma((2, 4)),
                dma((2, GROUPS - 1)),
                dma((2, GROUPS - 1)),
            ],
            compiler_params=pltpu.CompilerParams(
                collective_id=0, has_side_effects=True, vmem_limit_bytes=48 << 20
            ),
        )(doc_lengths, flat(queries), flat(output), flat(grad_output), flat(keys), flat(values))
        return (
            dq.reshape(queries.shape),
            dk.reshape(keys.shape),
            dv.reshape(values.shape),
        )

    return jax.shard_map(
        body,
        mesh=mesh,
        in_specs=(
            P("ctx", "head", None),
            P(("ctx", "head"), None, None),
            P(("ctx", "head"), None, None),
            P("ctx", "head", None),
            P("ctx", "head", None),
            P(),
        ),
        out_specs=(
            P("ctx", "head", None),
            P(("ctx", "head"), None, None),
            P(("ctx", "head"), None, None),
        ),
        check_vma=False,
    )
```

time: 201 us -> 56.1 us (0.28)
  the two profiles are of different devices: /device:TPU:14 before, /device:TPU:1 now
where the time goes in v1:
time: 56.1 us; the launch traced here: 55.8 us
  Pallas kernels  47.7 us (85%)
  local copies, waits for them, and re-layouts  7.5 us (13%)
  between operations  0.65 us (1%)
    pallas_call x1, Pallas kernels, body(): pl.pallas_call(functools.partial(kernel, n_ctx), out_shape=(jax.ShapeDtyp...  47.7 us
    unnamed x15, local copies, waits for them, and re-layouts  7.5 us

profile of v1, /device:TPU:1, one launch (start us, length us, event | category | flops | bytes accessed | tf_op | source)
XLA Modules:
  0.0 55.8 jit_solution(8261241463650339993)
XLA Ops:
  0.6 0.0 copy-start.5
  0.6 0.6 %copy-done.5 = s32[16]{0:T(128)S(1)} copy-done((s32[16]{0:T(128)S(1)}, s32[16]{0:T(128)}, u32[]{:S(2)}) %copy-start.5) | copy-done | bytes 88
  1.3 0.0 copy-start
  1.3 1.0 %copy-done = bf16[256,8,128]{2,1,0:T(8,128)(2,1)S(1)} copy-done((bf16[256,8,128]{2,1,0:T(8,128)(2,1)S(1)}, bf16[256,8,128]{2,1,0:T(8,128)(2,1)}, u32[]{:S(2)}) %copy-start) | copy-done | bytes 524312
  2.3 0.0 copy-start.1
  2.3 1.0 %copy-done.1 = bf16[256,8,128]{2,1,0:T(8,128)(2,1)S(1)} copy-done((bf16[256,8,128]{2,1,0:T(8,128)(2,1)S(1)}, bf16[256,8,128]{2,1,0:T(8,128)(2,1)}, u32[]{:S(2)}) %copy-start.1) | copy-done | bytes 524312
  3.4 0.0 copy-start.2
  3.4 1.0 %copy-done.2 = bf16[256,8,128]{2,1,0:T(8,128)(2,1)S(1)} copy-done((bf16[256,8,128]{2,1,0:T(8,128)(2,1)S(1)}, bf16[256,8,128]{2,1,0:T(8,128)(2,1)}, u32[]{:S(2)}) %copy-start.2) | copy-done | bytes 524312
  4.4 0.0 copy-start.3
  4.4 0.8 %copy-done.3 = bf16[32,8,128]{2,1,0:T(8,128)(2,1)S(1)} copy-done((bf16[32,8,128]{2,1,0:T(8,128)(2,1)S(1)}, bf16[32,8,128]{2,1,0:T(8,128)(2,1)}, u32[]{:S(2)}) %copy-start.3) | copy-done | bytes 65560
  5.3 0.0 copy-start.4
  5.3 0.8 %copy-done.4 = bf16[32,8,128]{2,1,0:T(8,128)(2,1)S(1)} copy-done((bf16[32,8,128]{2,1,0:T(8,128)(2,1)S(1)}, bf16[32,8,128]{2,1,0:T(8,128)(2,1)}, u32[]{:S(2)}) %copy-start.4) | copy-done | bytes 65560
  6.1 47.7 %shard_map.85 = (bf16[2048,128]{1,0:T(8,128)(2,1)S(1)}, bf16[256,128]{1,0:T(8,128)(2,1)S(1)}, bf16[256,128]{1,0:T(8,128)(2,1)S(1)}) custom-call(s32[16]{0:T(128)S(1)} %copy-done.5, bf16[2048,128]{1,0:T(8,128)(2,1)S(1)} %bitcast.8, bf16[2048,128]{1,0:T(8,128)(2,1)S(1)} %bitcast.9, bf16[2048,128]{1,0:T(8,128)(2,1)S(1)} %bitcast.10, ...), custom_call_target="tpu_custom_call" | custom-call | tf_op jit(solution)/shard_map/pallas_call | solution.py:351
  53.8 0.8 %copy.12 = bf16[256,8,128]{2,1,0:T(8,128)(2,1)} copy(bf16[256,8,128]{2,1,0:T(8,128)(2,1)S(1)} %bitcast.11) | data formatting | bytes 1048576
  54.6 0.6 %copy.13 = bf16[32,8,128]{2,1,0:T(8,128)(2,1)} copy(bf16[32,8,128]{2,1,0:T(8,128)(2,1)S(1)} %bitcast.15) | data formatting | bytes 131072
  55.2 0.6 %copy.14 = bf16[32,8,128]{2,1,0:T(8,128)(2,1)} copy(bf16[32,8,128]{2,1,0:T(8,128)(2,1)S(1)} %bitcast.14) | data formatting | bytes 131072
Async XLA Ops:
  0.6 0.7 %copy-start.5 = (s32[16]{0:T(128)S(1)}, s32[16]{0:T(128)}, u32[]{:S(2)}) copy-start(s32[16]{0:T(128)} %lens_ref.1) | copy-start | bytes 196
  1.3 1.0 %copy-start = (bf16[256,8,128]{2,1,0:T(8,128)(2,1)S(1)}, bf16[256,8,128]{2,1,0:T(8,128)(2,1)}, u32[]{:S(2)}) copy-start(bf16[256,8,128]{2,1,0:T(8,128)(2,1)} %param.6) | copy-start | bytes 1572868
  2.3 1.0 %copy-start.1 = (bf16[256,8,128]{2,1,0:T(8,128)(2,1)S(1)}, bf16[256,8,128]{2,1,0:T(8,128)(2,1)}, u32[]{:S(2)}) copy-start(bf16[256,8,128]{2,1,0:T(8,128)(2,1)} %param.9) | copy-start | bytes 1572868
  3.4 1.0 %copy-start.2 = (bf16[256,8,128]{2,1,0:T(8,128)(2,1)S(1)}, bf16[256,8,128]{2,1,0:T(8,128)(2,1)}, u32[]{:S(2)}) copy-start(bf16[256,8,128]{2,1,0:T(8,128)(2,1)} %param.10) | copy-start | bytes 1572868
  4.4 0.8 %copy-start.3 = (bf16[32,8,128]{2,1,0:T(8,128)(2,1)S(1)}, bf16[32,8,128]{2,1,0:T(8,128)(2,1)}, u32[]{:S(2)}) copy-start(bf16[32,8,128]{2,1,0:T(8,128)(2,1)} %param.7) | copy-start | bytes 196612
  5.3 0.8 %copy-start.4 = (bf16[32,8,128]{2,1,0:T(8,128)(2,1)S(1)}, bf16[32,8,128]{2,1,0:T(8,128)(2,1)}, u32[]{:S(2)}) copy-start(bf16[32,8,128]{2,1,0:T(8,128)(2,1)} %param.8) | copy-start | bytes 196612

commit v2 on v1

v2 whole, which is shorter than its diff:
```python
import functools
import math

import jax
import jax.numpy as jnp
from jax import lax
from jax.experimental import pallas as pl
from jax.experimental.pallas import tpu as pltpu
from jax.sharding import PartitionSpec as P

MESH = pl.DeviceIdType.MESH
F32 = jnp.float32
BF16 = jnp.bfloat16

BLOCK = 256
REACH = 4
WINDOW = (REACH + 1) * BLOCK
WIDTH = 128
HEADS = 8
GROUPS = 8
ROWS = BLOCK * HEADS
TILE = 256
TILES = ROWS // TILE
STEP = TILE // HEADS
PIECE = BLOCK // GROUPS
NDOCS = 16
FAR = 2.0**20
SCALE = 1.0 / math.sqrt(WIDTH)
RATE = SCALE / math.log(2.0)

HALF = BLOCK // 2


def reach(s, t):
    if s == REACH:
        return (0, HALF) if t < TILES // 2 else (0, BLOCK)
    if s == 0 and t >= TILES // 2:
        return (HALF, BLOCK)
    return (0, BLOCK)


def halves(s):
    if s == REACH:
        return ((0, HALF, 0, ROWS), (HALF, BLOCK, ROWS // 2, ROWS))
    if s == 0:
        return ((0, HALF, 0, ROWS // 2), (HALF, BLOCK, 0, ROWS))
    return ((0, BLOCK, 0, ROWS),)


VMEM = (64 << 20) - (640 << 10)

NT = (((1,), (1,)), ((), ()))
NN = (((1,), (0,)), ((), ()))
TN = (((0,), (0,)), ((), ()))


def dot(a, b, dims=NN):
    return lax.dot_general(a, b, dims, preferred_element_type=F32)


def iota(shape, dim):
    return lax.broadcasted_iota(jnp.int32, shape, dim)


def kernel(
    n_ctx,
    lens_any, q_any, o_any, g_any, k_any, v_any,
    dq_any, fin_any,
    dq_ref, lens_ref, q_ref, o_ref, g_ref, k_ref, v_ref,
    kb, vb, order, kp, vp, kaug, qaug, gt, delta, band, m_st, l_st, w_st, wd_st,
    gw, dka, dva, stage, got, sent,
    in_sem, out_sem, ks_sem, kr_sem, vs_sem, vr_sem, cs_sem, cr_sem, rs_sem, rr_sem, fs_sem, fr_sem,
):
    c = lax.axis_index("ctx")
    z = lax.axis_index("head")
    core = lax.rem(c, 2)
    sib = c + 1 - 2 * core
    ahead = {o: lax.rem(c + o, n_ctx) for o in (1, 2, 4)}
    behind = {o: lax.rem(c + n_ctx - o, n_ctx) for o in (1, 2, 4)}
    peers = [lax.rem(z + o, GROUPS) for o in range(1, GROUPS)]

    barrier = pltpu.get_barrier_semaphore()
    for peer in peers:
        pl.semaphore_signal(barrier, inc=1, device_id={"head": peer}, device_id_type=MESH)
    for other in (*ahead.values(), *behind.values()):
        pl.semaphore_signal(barrier, inc=1, device_id={"ctx": other}, device_id_type=MESH)

    loads = []
    for i, (source, target) in enumerate(
        (
            (k_any, k_ref), (v_any, v_ref), (lens_any, lens_ref),
            (q_any, q_ref), (g_any, g_ref), (o_any, o_ref),
        )
    ):
        load = pltpu.make_async_copy(source, target, in_sem.at[i])
        load.start()
        loads.append(load)
    row, col = iota((BLOCK, BLOCK), 0), iota((BLOCK, BLOCK), 1)
    order[...] = jnp.where(
        col == (row % PIECE) * GROUPS + row // PIECE, 1.0, 0.0
    ).astype(BF16)
    mine = pl.multiple_of(PIECE * z, PIECE)
    k_copies, v_copies = [], []
    for i, (given, piece, window, send, recv, copies) in enumerate(
        (
            (k_ref, kp, kb, ks_sem, kr_sem, k_copies),
            (v_ref, vp, vb, vs_sem, vr_sem, v_copies),
        )
    ):
        loads[i].wait()
        piece[...] = dot(order[...], given[...]).astype(BF16)
        if i == 0:
            pl.semaphore_wait(barrier, GROUPS - 1 + len(ahead) + len(behind))
        for o, peer in enumerate(peers):
            copy = pltpu.make_async_remote_copy(
                src_ref=piece.at[pl.ds(pl.multiple_of(PIECE * peer, PIECE), PIECE)],
                dst_ref=window.at[pl.ds(pl.multiple_of(REACH * BLOCK + mine, PIECE), PIECE)],
                send_sem=send.at[o],
                recv_sem=recv.at[o],
                device_id={"head": peer},
                device_id_type=MESH,
            )
            copy.start()
            copies.append(copy)
        window[pl.ds(pl.multiple_of(REACH * BLOCK + mine, PIECE), PIECE), :] = piece[pl.ds(mine, PIECE), :]

    for load in loads[2:]:
        load.wait()
    lane = iota((1, WIDTH), 1)
    start = jnp.int32(0)
    starts = jnp.full((1, WIDTH), 1 << 30, jnp.int32)
    ends = jnp.full((1, WIDTH), 1 << 30, jnp.int32)
    for doc in range(NDOCS):
        end = start + lens_ref[doc]
        starts = jnp.where(lane == doc, start, starts)
        ends = jnp.where(lane == doc, end, ends)
        start = end
    starts = jnp.where(lane == NDOCS, -(1 << 30), starts)
    ends = jnp.where(lane == NDOCS, 0, ends)

    key_pos = (c - REACH) * BLOCK + iota((WINDOW, WIDTH), 0)
    kaug[...] = jnp.where((starts <= key_pos) & (key_pos < ends), 1.0, 0.0).astype(BF16)
    row_pos = c * BLOCK + lax.shift_right_logical(iota((ROWS, WIDTH), 0), 3)
    outside = jnp.where((starts <= row_pos) & (row_pos < ends), 0.0, -FAR)
    qaug[...] = jnp.where(iota((ROWS, WIDTH), 1) <= NDOCS, outside, 0.0).astype(BF16)

    for t in range(TILES):
        g_t = jnp.transpose(g_ref[pl.ds(TILE * t, TILE), :])
        o_t = jnp.transpose(o_ref[pl.ds(TILE * t, TILE), :])
        gt[:, pl.ds(TILE * t, TILE)] = g_t
        delta[pl.ds(t, 1), :] = jnp.sum(
            g_t.astype(F32) * o_t.astype(F32), axis=0, keepdims=True
        )

    def ahead_by(window, i, o, other):
        return pltpu.make_async_remote_copy(
            src_ref=window.at[pl.ds(REACH * BLOCK, BLOCK)],
            dst_ref=window.at[pl.ds((REACH - o) * BLOCK, BLOCK)],
            send_sem=cs_sem.at[i, o // 2],
            recv_sem=cr_sem.at[i, o // 2],
            device_id={"ctx": other},
            device_id_type=MESH,
        )

    def aside(window, i, hop):
        at = (REACH - 2 * hop) * BLOCK - 2 * BLOCK * core
        return pltpu.make_async_remote_copy(
            src_ref=window.at[pl.ds(pl.multiple_of(at, BLOCK), BLOCK)],
            dst_ref=window.at[pl.ds((REACH - 2 * hop - 1) * BLOCK, BLOCK)],
            send_sem=cs_sem.at[i, 3 * hop],
            recv_sem=cr_sem.at[i, 3 * hop],
            device_id={"ctx": sib},
            device_id_type=MESH,
        )

    k_ahead = {o: ahead_by(kb, 0, o, ahead[o]) for o in (1, 2, 4)}
    v_ahead = {o: ahead_by(vb, 1, o, ahead[o]) for o in (2, 4)}
    k_side = aside(kb, 0, 1)
    v_side = [aside(vb, 1, hop) for hop in range(2)]

    def scores(s):
        for t in range(TILES):
            lo, hi = reach(s, t)
            at = pl.ds(BLOCK * s + lo, hi - lo)
            here = pl.ds(TILE * t, TILE)
            left = jnp.concatenate([kb[at, :], kaug[at, :]], axis=1)
            right = jnp.concatenate([q_ref[here, :], qaug[here, :]], axis=1)
            x = dot(left, right, NT)
            if s == REACH:
                key = hi - HALF + iota((HALF, TILE), 0)
                query = STEP * t + lax.shift_right_logical(iota((HALF, TILE), 1), 3)
                own = jnp.where(key <= query, x[hi - HALF :], -1e30)
                x = own if hi == HALF else jnp.concatenate([x[:HALF], own], axis=0)
            m = jnp.max(x, axis=0, keepdims=True)
            e = jnp.exp2((x - m) * RATE)
            m_st[s, pl.ds(t, 1), :] = m
            l_st[s, pl.ds(t, 1), :] = jnp.sum(e, axis=0, keepdims=True)
            band[at, here] = e.astype(BF16)

    for copy in k_copies:
        copy.wait_recv()
    for o in (1, 2, 4):
        k_ahead[o].start()
    for copy in v_copies:
        copy.wait_recv()

    @pl.when(core == 0)
    def _():
        v_side[0].start()

    scores(4)
    k_ahead[1].wait_recv()
    scores(3)
    k_ahead[2].wait_recv()

    @pl.when(core == 0)
    def _():
        k_side.start()

    k_ahead[4].wait_recv()

    @pl.when(core == 1)
    def _():
        k_side.start()

    for o in (2, 4):
        v_ahead[o].start()
    scores(2)
    scores(0)
    k_side.wait_recv()
    scores(1)

    slots = range(REACH + 1)
    top = functools.reduce(jnp.maximum, [m_st[s] for s in slots])
    parts = [jnp.exp2((m_st[s] - top) * RATE) for s in slots]
    total = sum(part * l_st[s] for s, part in enumerate(parts))
    for s, part in enumerate(parts):
        share = part / total
        w_st[s] = share
        wd_st[s] = share * delta[...]

    def value_grads(s):
        for t in range(TILES):
            here = pl.ds(TILE * t, TILE)
            gw[s, :, here] = (gt[:, here].astype(F32) * w_st[s, pl.ds(t, 1), :]).astype(BF16)
        for lo, hi, first, end in halves(s):
            at, rows = pl.ds(BLOCK * s + lo, hi - lo), pl.ds(first, end - first)
            dva[at, :] = dot(band[at, rows], gw[s, :, rows], NT)

    def key_grads(s):
        for t in range(TILES):
            lo, hi = reach(s, t)
            at = pl.ds(BLOCK * s + lo, hi - lo)
            here = pl.ds(TILE * t, TILE)
            dp = dot(vb[at, :], gw[s, :, here])
            band[at, here] = band[at, here] * (dp - wd_st[s, pl.ds(t, 1), :]).astype(BF16)
        for lo, hi, first, end in halves(s):
            at, rows = pl.ds(BLOCK * s + lo, hi - lo), pl.ds(first, end - first)
            dka[at, :] = dot(band[at, rows], q_ref[rows, :])

    def back(i, hop, other):
        return pltpu.make_async_remote_copy(
            src_ref=stage.at[i, hop],
            dst_ref=got.at[i, hop],
            send_sem=rs_sem.at[i, hop],
            recv_sem=rr_sem.at[i, hop],
            device_id={"ctx": other},
            device_id_type=MESH,
        )

    accs = (dva, dka)
    returns = [
        [back(i, hop, other) for hop, other in enumerate((sib, behind[1], behind[2], behind[4]))]
        for i in range(2)
    ]

    def hand(i, hop, s, extra):
        value = accs[i][pl.ds(BLOCK * s, BLOCK), :]
        if extra:
            value = value + got[i, 0].astype(F32)
        stage[i, hop] = value.astype(BF16)
        returns[i][hop].start()

    def grads(i, part, between=((), ())):
        part(0)

        @pl.when(core == 0)
        def _():
            hand(i, 3, 0, False)

        for step in between[0]:
            step()
        part(1)
        hand(i, 0, 1, False)
        for step in between[1]:
            step()
        part(2)

        @pl.when(core == 1)
        def _():
            hand(i, 2, 2, False)

        part(3)
        hand(i, 1, 3, False)
        returns[i][0].wait_recv()

        @pl.when(core == 0)
        def _():
            hand(i, 2, 2, True)

        @pl.when(core == 1)
        def _():
            hand(i, 3, 0, True)

        part(4)

    def relay_near():
        v_ahead[2].wait_recv()

        @pl.when(core == 0)
        def _():
            v_side[1].start()

        @pl.when(core == 1)
        def _():
            v_side[0].start()

    def relay_far():
        v_ahead[4].wait_recv()

        @pl.when(core == 1)
        def _():
            v_side[1].start()

    last = []

    def finish(i):
        for hop in (3, 2, 1):
            returns[i][hop].wait_recv()
        whole = accs[i][pl.ds(REACH * BLOCK, BLOCK), :]
        for hop in (1, 2, 3):
            whole = whole + got[i, hop].astype(F32)
        if i == 1:
            whole = whole * SCALE
        sent[i] = whole.astype(BF16)
        for o, peer in enumerate(peers):
            copy = pltpu.make_async_remote_copy(
                src_ref=sent.at[i, pl.ds(pl.multiple_of(PIECE * peer, PIECE), PIECE)],
                dst_ref=fin_any.at[i, pl.ds(mine, PIECE)],
                send_sem=fs_sem.at[i, o],
                recv_sem=fr_sem.at[i, o],
                device_id={"head": peer},
                device_id_type=MESH,
            )
            copy.start()
            last.append(copy)
        save = pltpu.make_async_copy(
            sent.at[i, pl.ds(mine, PIECE)], fin_any.at[i, pl.ds(mine, PIECE)], out_sem.at[i]
        )
        save.start()
        saves.append(save)

    saves = []
    grads(0, value_grads, ((relay_near,), (relay_far,)))
    for copy in v_side:
        copy.wait_recv()
    grads(1, key_grads)
    finish(0)

    for t in range(TILES):
        here = pl.ds(TILE * t, TILE)
        first, end = reach(0, t)[0], REACH * BLOCK + reach(REACH, t)[1]
        at = pl.ds(first, end - first)
        dq_ref[here, :] = (dot(band[at, here], kb[at, :], TN) * SCALE).astype(BF16)

    save = pltpu.make_async_copy(dq_ref, dq_any, out_sem.at[2])
    save.start()
    saves.append(save)
    finish(1)

    for copy in last:
        copy.wait_recv()
    for copy in (*k_copies, *v_copies, *k_ahead.values(), *v_ahead.values(), k_side, *v_side):
        copy.wait_send()
    for copy in (*returns[0], *returns[1], *last):
        copy.wait_send()
    for save in saves:
        save.wait()


PARTS = 4


def store(dq_any, fin_any, dq_out, dk_out, dv_out, dq_ref, fin, dk_ref, dv_ref, load_sem, save_sem):
    part = [pl.ds(ROWS // PARTS * i, ROWS // PARTS) for i in range(PARTS)]
    loads = [pltpu.make_async_copy(fin_any, fin, load_sem.at[PARTS])] + [
        pltpu.make_async_copy(dq_any.at[p], dq_ref.at[p], load_sem.at[i]) for i, p in enumerate(part)
    ]
    for load in loads:
        load.start()
    row, col = iota((BLOCK, BLOCK), 0), iota((BLOCK, BLOCK), 1)
    place = jnp.where(
        row == (col % PIECE) * GROUPS + col // PIECE, 1.0, 0.0
    ).astype(BF16)
    saves = []

    def save(source, target):
        copy = pltpu.make_async_copy(source, target, save_sem.at[len(saves)])
        copy.start()
        saves.append(copy)

    loads[0].wait()
    for i, (ref, out) in enumerate(((dv_ref, dv_out), (dk_ref, dk_out))):
        ref[...] = dot(place, fin[i]).astype(BF16)
        save(ref, out)
    for load, p in zip(loads[1:], part):
        load.wait()
        save(dq_ref.at[p], dq_out.at[p])
    for copy in saves:
        copy.wait()


def solution(mesh):
    n_ctx = mesh.shape["ctx"]
    dma = pltpu.SemaphoreType.DMA

    def body(queries, keys, values, output, grad_output, doc_lengths):
        flat = lambda x: x.reshape(-1, WIDTH)
        piece = PIECE * GROUPS
        dq, fin = pl.pallas_call(
            functools.partial(kernel, n_ctx),
            out_shape=(
                jax.ShapeDtypeStruct((ROWS, WIDTH), BF16),
                jax.ShapeDtypeStruct((2, piece, WIDTH), BF16),
            ),
            in_specs=[pl.BlockSpec(memory_space=pl.ANY)] * 6,
            out_specs=[pl.BlockSpec(memory_space=pl.ANY)] * 2,
            scratch_shapes=[
                pltpu.VMEM((ROWS, WIDTH), BF16),
                pltpu.SMEM((NDOCS,), jnp.int32),
                pltpu.VMEM((ROWS, WIDTH), BF16),
                pltpu.VMEM((ROWS, WIDTH), BF16),
                pltpu.VMEM((ROWS, WIDTH), BF16),
                pltpu.VMEM((piece, WIDTH), BF16),
                pltpu.VMEM((piece, WIDTH), BF16),
                pltpu.VMEM((WINDOW, WIDTH), BF16),
                pltpu.VMEM((WINDOW, WIDTH), BF16),
                pltpu.VMEM((BLOCK, BLOCK), BF16),
                pltpu.VMEM((piece, WIDTH), BF16),
                pltpu.VMEM((piece, WIDTH), BF16),
                pltpu.VMEM((WINDOW, WIDTH), BF16),
                pltpu.VMEM((ROWS, WIDTH), BF16),
                pltpu.VMEM((WIDTH, ROWS), BF16),
                pltpu.VMEM((TILES, TILE), F32),
                pltpu.VMEM((WINDOW, ROWS), BF16),
                pltpu.VMEM((REACH + 1, TILES, TILE), F32),
                pltpu.VMEM((REACH + 1, TILES, TILE), F32),
                pltpu.VMEM((REACH + 1, TILES, TILE), F32),
                pltpu.VMEM((REACH + 1, TILES, TILE), F32),
                pltpu.VMEM((REACH + 1, WIDTH, ROWS), BF16),
                pltpu.VMEM((WINDOW, WIDTH), F32),
                pltpu.VMEM((WINDOW, WIDTH), F32),
                pltpu.VMEM((2, 4, BLOCK, WIDTH), BF16),
                pltpu.VMEM((2, 4, BLOCK, WIDTH), BF16),
                pltpu.VMEM((2, BLOCK, WIDTH), BF16),
                dma((6,)),
                dma((3,)),
                dma((GROUPS - 1,)),
                dma((GROUPS - 1,)),
                dma((GROUPS - 1,)),
                dma((GROUPS - 1,)),
                dma((2, 4)),
                dma((2, 4)),
                dma((2, 4)),
                dma((2, 4)),
                dma((2, GROUPS - 1)),
                dma((2, GROUPS - 1)),
            ],
            compiler_params=pltpu.CompilerParams(
                collective_id=0, has_side_effects=True, vmem_limit_bytes=VMEM
            ),
        )(doc_lengths, flat(queries), flat(output), flat(grad_output), flat(keys), flat(values))
        dq, dk, dv = pl.pallas_call(
            store,
            out_shape=(
                jax.ShapeDtypeStruct((ROWS, WIDTH), BF16),
                jax.ShapeDtypeStruct((piece, WIDTH), BF16),
                jax.ShapeDtypeStruct((piece, WIDTH), BF16),
            ),
            in_specs=[pl.BlockSpec(memory_space=pl.ANY)] * 2,
            out_specs=[pl.BlockSpec(memory_space=pl.ANY)] * 3,
            scratch_shapes=[
                pltpu.VMEM((ROWS, WIDTH), BF16),
                pltpu.VMEM((2, piece, WIDTH), BF16),
                pltpu.VMEM((piece, WIDTH), BF16),
                pltpu.VMEM((piece, WIDTH), BF16),
                dma((PARTS + 1,)),
                dma((PARTS + 2,)),
            ],
            compiler_params=pltpu.CompilerParams(vmem_limit_bytes=VMEM),
        )(dq, fin)
        return (
            dq.reshape(queries.shape),
            dk.reshape(keys.shape),
            dv.reshape(values.shape),
        )

    return jax.shard_map(
        body,
        mesh=mesh,
        in_specs=(
            P("ctx", "head", None),
            P(("ctx", "head"), None, None),
            P(("ctx", "head"), None, None),
            P("ctx", "head", None),
            P("ctx", "head", None),
            P(),
        ),
        out_specs=(
            P("ctx", "head", None),
            P(("ctx", "head"), None, None),
            P(("ctx", "head"), None, None),
        ),
        check_vma=False,
    )
```

time: 56.1 us -> 43.8 us (0.78)
  local copies, waits for them, and re-layouts: 7.5 us -> 0 us
  Pallas kernels: 47.7 us -> 43 us
    unnamed x15 -> x0, local copies, waits for them, and re-layouts: 7.5 us -> none
    pallas_call x1, Pallas kernels: 47.7 us -> 41 us  [body(): pl.pallas_call(functools.partial(kernel, n_ctx), out_shape=(jax.ShapeDtyp...]
    pallas_call x0 -> x1, Pallas kernels: none -> 2.04 us  [body(): pl.pallas_call(store, out_shape=(jax.ShapeDtypeStruct((ROWS, WIDTH), BF16...]
where the time goes in v2:
time: 43.8 us; the launch traced here: 43.7 us
  Pallas kernels  43 us (98%)
  between operations  0.64 us (1%)
    pallas_call x1, Pallas kernels, body(): pl.pallas_call(functools.partial(kernel, n_ctx), out_shape=(jax.ShapeDtyp...  41 us
    pallas_call x1, Pallas kernels, body(): pl.pallas_call(store, out_shape=(jax.ShapeDtypeStruct((ROWS, WIDTH), BF16...  2.04 us

profile of v2, /device:TPU:1, one launch (start us, length us, event | category | flops | bytes accessed | tf_op | source)
XLA Modules:
  0.0 43.7 jit_solution(1705799476556322733)
XLA Ops:
  0.6 41.0 %shard_map.85 = (bf16[2048,128]{1,0:T(8,128)(2,1)}, bf16[2,256,128]{2,1,0:T(8,128)(2,1)}) custom-call(s32[16]{0:T(128)} %lens_any.1, bf16[2048,128]{1,0:T(8,128)(2,1)} %bitcast.8, bf16[2048,128]{1,0:T(8,128)(2,1)} %bitcast.9, bf16[2048,128]{1,0:T(8,128)(2,1)} %bitcast.10, bf16[256,128]{1,0:T(8,128)(2,1)} %bitcast.11, bf16[256,128]{1,0:T(8,128)(2,1)} %bitcast.12), custom_call_target="tpu_custom_call" | custom-call | tf_op jit(solution)/shard_map/pallas_call | solution.py:430
  41.6 2.0 %shard_map.86 = (bf16[2048,128]{1,0:T(8,128)(2,1)}, bf16[256,128]{1,0:T(8,128)(2,1)}, bf16[256,128]{1,0:T(8,128)(2,1)}) custom-call(bf16[2048,128]{1,0:T(8,128)(2,1)} %get-tuple-element.8.dq_any, bf16[2,256,128]{2,1,0:T(8,128)(2,1)} %get-tuple-element.9.fin_any), custom_call_target="tpu_custom_call" | custom-call | tf_op jit(solution)/shard_map/pallas_call | solution.py:483

commit v3 on v2

--- a/solution.py
+++ b/solution.py
@@ -77,24 +77,27 @@
     sib = c + 1 - 2 * core
     ahead = {o: lax.rem(c + o, n_ctx) for o in (1, 2, 4)}
     behind = {o: lax.rem(c + n_ctx - o, n_ctx) for o in (1, 2, 4)}
-    peers = [lax.rem(z + o, GROUPS) for o in range(1, GROUPS)]
-
+    peers = [lax.rem(z + o, GROUPS) for o in (4, 3, 5, 2, 6, 1, 7)]
+
+    loads = []
+    for i, (source, target) in enumerate(
+        (
+            (k_any, k_ref), (v_any, v_ref), (lens_any, lens_ref),
+            (q_any, q_ref), (g_any, g_ref), (o_any, o_ref),
+        )
+    ):
+        load = pltpu.make_async_copy(source, target, in_sem.at[i])
+        loads.append(load)
+    loads[0].start()
+    loads[1].start()
     barrier = pltpu.get_barrier_semaphore()
     for peer in peers:
         pl.semaphore_signal(barrier, inc=1, device_id={"head": peer}, device_id_type=MESH)
     for other in (*ahead.values(), *behind.values()):
         pl.semaphore_signal(barrier, inc=1, device_id={"ctx": other}, device_id_type=MESH)
 
-    loads = []
-    for i, (source, target) in enumerate(
-        (
-            (k_any, k_ref), (v_any, v_ref), (lens_any, lens_ref),
-            (q_any, q_ref), (g_any, g_ref), (o_any, o_ref),
-        )
-    ):
-        load = pltpu.make_async_copy(source, target, in_sem.at[i])
+    for load in loads[2:]:
         load.start()
-        loads.append(load)
     row, col = iota((BLOCK, BLOCK), 0), iota((BLOCK, BLOCK), 1)
     order[...] = jnp.where(
         col == (row % PIECE) * GROUPS + row // PIECE, 1.0, 0.0
@@ -173,9 +176,9 @@
             device_id_type=MESH,
         )
 
-    k_ahead = {o: ahead_by(kb, 0, o, ahead[o]) for o in (1, 2, 4)}
+    k_ahead = {o: ahead_by(kb, 0, o, ahead[o]) for o in (2, 4)}
     v_ahead = {o: ahead_by(vb, 1, o, ahead[o]) for o in (2, 4)}
-    k_side = aside(kb, 0, 1)
+    k_side = [aside(kb, 0, hop) for hop in range(2)]
     v_side = [aside(vb, 1, hop) for hop in range(2)]
 
     def scores(s):
@@ -197,10 +200,33 @@
             l_st[s, pl.ds(t, 1), :] = jnp.sum(e, axis=0, keepdims=True)
             band[at, here] = e.astype(BF16)
 
+    def relay_near(arrived, handed):
+        arrived[2].wait_recv()
+
+        @pl.when(core == 0)
+        def _():
+            handed[1].start()
+
+        @pl.when(core == 1)
+        def _():
+            handed[0].start()
+
+    def relay_far(arrived, handed):
+        arrived[4].wait_recv()
+
+        @pl.when(core == 1)
+        def _():
+            handed[1].start()
+
     for copy in k_copies:
         copy.wait_recv()
-    for o in (1, 2, 4):
+    for o in (2, 4):
         k_ahead[o].start()
+
+    @pl.when(core == 0)
+    def _():
+        k_side[0].start()
+
     for copy in v_copies:
         copy.wait_recv()
 
@@ -209,26 +235,17 @@
         v_side[0].start()
 
     scores(4)
-    k_ahead[1].wait_recv()
-    scores(3)
-    k_ahead[2].wait_recv()
-
-    @pl.when(core == 0)
-    def _():
-        k_side.start()
-
-    k_ahead[4].wait_recv()
-
-    @pl.when(core == 1)
-    def _():
-        k_side.start()
-
     for o in (2, 4):
         v_ahead[o].start()
+    relay_near(k_ahead, k_side)
     scores(2)
+    relay_far(k_ahead, k_side)
     scores(0)
-    k_side.wait_recv()
+    k_side[0].wait_recv()
+    scores(3)
+    k_side[1].wait_recv()
     scores(1)
+    relay_near(v_ahead, v_side)
 
     slots = range(REACH + 1)
     top = functools.reduce(jnp.maximum, [m_st[s] for s in slots])
@@ -281,56 +298,26 @@
         stage[i, hop] = value.astype(BF16)
         returns[i][hop].start()
 
-    def grads(i, part, between=((), ())):
-        part(0)
+    def sums(i):
+        returns[i][0].wait_recv()
 
         @pl.when(core == 0)
         def _():
+            hand(i, 2, 2, True)
+
+        @pl.when(core == 1)
+        def _():
+            hand(i, 3, 0, True)
+
+    def far_of_one(i):
+        @pl.when(core == 1)
+        def _():
+            hand(i, 2, 2, False)
+
+    def farther_of_zero(i):
+        @pl.when(core == 0)
+        def _():
             hand(i, 3, 0, False)
-
-        for step in between[0]:
-            step()
-        part(1)
-        hand(i, 0, 1, False)
-        for step in between[1]:
-            step()
-        part(2)
-
-        @pl.when(core == 1)
-        def _():
-            hand(i, 2, 2, False)
-
-        part(3)
-        hand(i, 1, 3, False)
-        returns[i][0].wait_recv()
-
-        @pl.when(core == 0)
-        def _():
-            hand(i, 2, 2, True)
-
-        @pl.when(core == 1)
-        def _():
-            hand(i, 3, 0, True)
-
-        part(4)
-
-    def relay_near():
-        v_ahead[2].wait_recv()
-
-        @pl.when(core == 0)
-        def _():
-            v_side[1].start()
-
-        @pl.when(core == 1)
-        def _():
-            v_side[0].start()
-
-    def relay_far():
-        v_ahead[4].wait_recv()
-
-        @pl.when(core == 1)
-        def _():
-            v_side[1].start()
 
     last = []
 
@@ -361,10 +348,29 @@
         saves.append(save)
 
     saves = []
-    grads(0, value_grads, ((relay_near,), (relay_far,)))
-    for copy in v_side:
-        copy.wait_recv()
-    grads(1, key_grads)
+    value_grads(0)
+    farther_of_zero(0)
+    value_grads(1)
+    hand(0, 0, 1, False)
+    relay_far(v_ahead, v_side)
+    value_grads(2)
+    far_of_one(0)
+    value_grads(3)
+    hand(0, 1, 3, False)
+    sums(0)
+    key_grads(0)
+    farther_of_zero(1)
+    v_side[1].wait_recv()
+    key_grads(1)
+    hand(1, 0, 1, False)
+    key_grads(2)
+    far_of_one(1)
+    v_side[0].wait_recv()
+    key_grads(3)
+    hand(1, 1, 3, False)
+    sums(1)
+    value_grads(4)
+    key_grads(4)
     finish(0)
 
     for t in range(TILES):
@@ -380,7 +386,7 @@
 
     for copy in last:
         copy.wait_recv()
-    for copy in (*k_copies, *v_copies, *k_ahead.values(), *v_ahead.values(), k_side, *v_side):
+    for copy in (*k_copies, *v_copies, *k_ahead.values(), *v_ahead.values(), *k_side, *v_side):
         copy.wait_send()
     for copy in (*returns[0], *returns[1], *last):
         copy.wait_send()
@@ -388,7 +394,7 @@
         save.wait()
 
 
-PARTS = 4
+PARTS = 1
 
 
 def store(dq_any, fin_any, dq_out, dk_out, dv_out, dq_ref, fin, dk_ref, dv_ref, load_sem, save_sem):

time: 43.8 us -> 41.8 us (0.954)
  the two profiles are of different devices: /device:TPU:1 before, /device:TPU:30 now
where the time goes in v3:
time: 41.8 us; the launch traced here: 41.6 us
  Pallas kernels  41 us (98%)
  between operations  0.64 us (2%)
    pallas_call x1, Pallas kernels, body(): pl.pallas_call(functools.partial(kernel, n_ctx), out_shape=(jax.ShapeDtyp...  39 us
    pallas_call x1, Pallas kernels, body(): pl.pallas_call(store, out_shape=(jax.ShapeDtypeStruct((ROWS, WIDTH), BF16...  2 us

profile of v3, /device:TPU:30, one launch (start us, length us, event | category | flops | bytes accessed | tf_op | source)
XLA Modules:
  0.0 41.6 jit_solution(2528261529534304924)
XLA Ops:
  0.6 39.0 %shard_map.85 = (bf16[2048,128]{1,0:T(8,128)(2,1)}, bf16[2,256,128]{2,1,0:T(8,128)(2,1)}) custom-call(s32[16]{0:T(128)} %lens_any.1, bf16[2048,128]{1,0:T(8,128)(2,1)} %bitcast.8, bf16[2048,128]{1,0:T(8,128)(2,1)} %bitcast.9, bf16[2048,128]{1,0:T(8,128)(2,1)} %bitcast.10, bf16[256,128]{1,0:T(8,128)(2,1)} %bitcast.11, bf16[256,128]{1,0:T(8,128)(2,1)} %bitcast.12), custom_call_target="tpu_custom_call" | custom-call | tf_op jit(solution)/shard_map/pallas_call | solution.py:436
  39.6 2.0 %shard_map.86 = (bf16[2048,128]{1,0:T(8,128)(2,1)}, bf16[256,128]{1,0:T(8,128)(2,1)}, bf16[256,128]{1,0:T(8,128)(2,1)}) custom-call(bf16[2048,128]{1,0:T(8,128)(2,1)} %get-tuple-element.8.dq_any, bf16[2,256,128]{2,1,0:T(8,128)(2,1)} %get-tuple-element.9.fin_any), custom_call_target="tpu_custom_call" | custom-call | tf_op jit(solution)/shard_map/pallas_call | solution.py:489

commit v4 on v3

--- a/solution.py
+++ b/solution.py
@@ -235,9 +235,9 @@
         v_side[0].start()
 
     scores(4)
-    for o in (2, 4):
-        v_ahead[o].start()
+    v_ahead[2].start()
     relay_near(k_ahead, k_side)
+    v_ahead[4].start()
     scores(2)
     relay_far(k_ahead, k_side)
     scores(0)

time: 41.8 us -> 41.3 us (0.988)
  Pallas kernels: 41 us -> 40.5 us
    pallas_call x1, Pallas kernels: 39 us -> 38.5 us  [body(): pl.pallas_call(functools.partial(kernel, n_ctx), out_shape=(jax.ShapeDtyp...]
where the time goes in v4:
time: 41.3 us; the launch traced here: 41.2 us
  Pallas kernels  40.5 us (98%)
  between operations  0.64 us (2%)
    pallas_call x1, Pallas kernels, body(): pl.pallas_call(functools.partial(kernel, n_ctx), out_shape=(jax.ShapeDtyp...  38.5 us
    pallas_call x1, Pallas kernels, body(): pl.pallas_call(store, out_shape=(jax.ShapeDtypeStruct((ROWS, WIDTH), BF16...  2 us

profile of v4, /device:TPU:30, one launch (start us, length us, event | category | flops | bytes accessed | tf_op | source)
XLA Modules:
  0.0 41.2 jit_solution(2625546721526161294)
XLA Ops:
  0.6 38.5 %shard_map.85 = (bf16[2048,128]{1,0:T(8,128)(2,1)}, bf16[2,256,128]{2,1,0:T(8,128)(2,1)}) custom-call(s32[16]{0:T(128)} %lens_any.1, bf16[2048,128]{1,0:T(8,128)(2,1)} %bitcast.8, bf16[2048,128]{1,0:T(8,128)(2,1)} %bitcast.9, bf16[2048,128]{1,0:T(8,128)(2,1)} %bitcast.10, bf16[256,128]{1,0:T(8,128)(2,1)} %bitcast.11, bf16[256,128]{1,0:T(8,128)(2,1)} %bitcast.12), custom_call_target="tpu_custom_call" | custom-call | tf_op jit(solution)/shard_map/pallas_call | solution.py:436
  39.2 2.0 %shard_map.86 = (bf16[2048,128]{1,0:T(8,128)(2,1)}, bf16[256,128]{1,0:T(8,128)(2,1)}, bf16[256,128]{1,0:T(8,128)(2,1)}) custom-call(bf16[2048,128]{1,0:T(8,128)(2,1)} %get-tuple-element.8.dq_any, bf16[2,256,128]{2,1,0:T(8,128)(2,1)} %get-tuple-element.9.fin_any), custom_call_target="tpu_custom_call" | custom-call | tf_op jit(solution)/shard_map/pallas_call | solution.py:489

commit v5 on v4

--- a/solution.py
+++ b/solution.py
@@ -220,7 +220,7 @@
 
     for copy in k_copies:
         copy.wait_recv()
-    for o in (2, 4):
+    for o in (4, 2):
         k_ahead[o].start()
 
     @pl.when(core == 0)

time: 41.3 us -> 42 us (1.017)
  Pallas kernels: 40.5 us -> 41.3 us
    pallas_call x1, Pallas kernels: 38.5 us -> 39.3 us  [body(): pl.pallas_call(functools.partial(kernel, n_ctx), out_shape=(jax.ShapeDtyp...]
where the time goes in v5:
time: 42 us; the launch traced here: 41.9 us
  Pallas kernels  41.3 us (98%)
  between operations  0.64 us (2%)
    pallas_call x1, Pallas kernels, body(): pl.pallas_call(functools.partial(kernel, n_ctx), out_shape=(jax.ShapeDtyp...  39.3 us
    pallas_call x1, Pallas kernels, body(): pl.pallas_call(store, out_shape=(jax.ShapeDtypeStruct((ROWS, WIDTH), BF16...  2 us

profile of v5, /device:TPU:30, one launch (start us, length us, event | category | flops | bytes accessed | tf_op | source)
XLA Modules:
  0.0 41.9 jit_solution(768855799103959718)
XLA Ops:
  0.6 39.3 %shard_map.85 = (bf16[2048,128]{1,0:T(8,128)(2,1)}, bf16[2,256,128]{2,1,0:T(8,128)(2,1)}) custom-call(s32[16]{0:T(128)} %lens_any.1, bf16[2048,128]{1,0:T(8,128)(2,1)} %bitcast.8, bf16[2048,128]{1,0:T(8,128)(2,1)} %bitcast.9, bf16[2048,128]{1,0:T(8,128)(2,1)} %bitcast.10, bf16[256,128]{1,0:T(8,128)(2,1)} %bitcast.11, bf16[256,128]{1,0:T(8,128)(2,1)} %bitcast.12), custom_call_target="tpu_custom_call" | custom-call | tf_op jit(solution)/shard_map/pallas_call | solution.py:436
  39.9 2.0 %shard_map.86 = (bf16[2048,128]{1,0:T(8,128)(2,1)}, bf16[256,128]{1,0:T(8,128)(2,1)}, bf16[256,128]{1,0:T(8,128)(2,1)}) custom-call(bf16[2048,128]{1,0:T(8,128)(2,1)} %get-tuple-element.8.dq_any, bf16[2,256,128]{2,1,0:T(8,128)(2,1)} %get-tuple-element.9.fin_any), custom_call_target="tpu_custom_call" | custom-call | tf_op jit(solution)/shard_map/pallas_call | solution.py:489
